TPU v7x, 32 devices: a whole 2x2x4 slice. The times are simulated.
32 devices in a mesh: pool: 16 (over z, y, core), tp: 2 (over x).
Axes of the slice: x: 2, y: 2, z: 4, core: 2. Of those that a mesh axis runs over, the one named last changes fastest.
Arguments:
- queries: bfloat16 [4096, 4096], P('pool', 'tp'), may hold values from -8 to 8
- new_key_values: bfloat16 [4096, 2048], P('pool', 'tp'), may hold values from -6 to 6
- key_value_store: bfloat16 [384, 256, 2048], P('pool', None, 'tp'), may hold values from -6 to 6
- o_weight: bfloat16 [4096, 8192], P('tp'), may hold values from -0.09375 to 0.09375
- residual: bfloat16 [4096, 8192], P(('pool', 'tp')), may hold values from -6 to 6
- hit_dev: int32 [32, 16], replicated, may hold values from 0 to 15, as said below
- hit_blk: int32 [32, 16], replicated, may hold values from 0 to 23
- prefix_len: int32 [32], replicated, may hold values from 3072 to 4096, as said below
Outputs:
- layer_out: bfloat16 [4096, 8192], P(('pool', 'tp'))
Inputs may be any that keep to these rules, and one draw needn't show every extreme that they name: `hit_dev`: within one request the 16 pool indices are distinct. So one pool index sends at most one used block to each request, and at most 2 to the 2 requests held by any one pool index. `prefix_len`: some request has the full 16 * 256 tokens.
All inputs are finite; a program needn't handle non-finite values.
Results may differ from a plain program's by a relative error of at most 0.0085.
Values may be sent and summed in bfloat16 or wider, within the bound.
No kernel may reach another device: no remote copies, remote signals or barrier semaphores. Data moves between devices by JAX's collectives and lax.ppermute only.
A program may use at most 192 MiB of HBM per device.

v0:
```python
import jax
import jax.numpy as jnp
from jax import lax
from jax.sharding import PartitionSpec as P

HEAD_SIZE = 128
NEW_TOKEN_COUNT = 128
PREFIX_BLOCK_LEN = 256
MAXB = 16


def shards(
    queries, new_key_values, key_value_store, o_weight, residual, hit_dev, hit_blk, prefix_len
):
    npool = lax.axis_size("pool")
    me = lax.axis_index("pool")
    rdev = queries.shape[0] // NEW_TOKEN_COUNT
    kv_local = key_value_store.shape[2] // (2 * HEAD_SIZE)
    q_local = queries.shape[1] // HEAD_SIZE
    query_group = q_local // kv_local
    token_span = MAXB * PREFIX_BLOCK_LEN
    dev_rows = hit_dev.reshape(npool, rdev, MAXB)
    blk_rows = hit_blk.reshape(npool, rdev, MAXB)
    starts = jnp.arange(MAXB, dtype=jnp.int32) * PREFIX_BLOCK_LEN
    used = starts[None, None, :] < prefix_len.reshape(npool, rdev)[:, :, None]
    match = used & (dev_rows == me)
    present = jnp.any(match, axis=2)
    chosen = jnp.sum(jnp.where(match, blk_rows, 0), axis=2)
    outgoing = jnp.take(key_value_store, chosen, axis=0)
    outgoing = jnp.where(present[:, :, None, None], outgoing, jnp.zeros_like(outgoing))
    outgoing = outgoing.reshape(npool, rdev, PREFIX_BLOCK_LEN, kv_local, 2, HEAD_SIZE)
    own_keys = outgoing[:, :, :, :, 0, :].reshape(
        npool, rdev, PREFIX_BLOCK_LEN, kv_local * HEAD_SIZE
    )
    own_values = outgoing[:, :, :, :, 1, :].reshape(
        npool, rdev, PREFIX_BLOCK_LEN, kv_local * HEAD_SIZE
    )
    base = me * rdev
    lengths = lax.dynamic_slice_in_dim(prefix_len, base, rdev, 0)
    sources = lax.dynamic_slice_in_dim(hit_dev, base, rdev, 0)
    fresh_tokens = new_key_values.reshape(rdev, NEW_TOKEN_COUNT, kv_local, 2, HEAD_SIZE)
    causal = (
        jnp.arange(NEW_TOKEN_COUNT, dtype=jnp.int32)[None, :]
        <= jnp.arange(NEW_TOKEN_COUNT, dtype=jnp.int32)[:, None]
    )

    def arrange(arrived, slot):
        ordered = jnp.take(arrived[:, slot], sources[slot], axis=0)
        return ordered.reshape(token_span, kv_local, HEAD_SIZE)

    outputs = []
    keys_in, values_in = (
        lax.all_to_all(own_keys, "pool", split_axis=0, concat_axis=0, tiled=True),
        lax.all_to_all(own_values, "pool", split_axis=0, concat_axis=0, tiled=True),
    )
    for slot in range(rdev):
        keys = arrange(keys_in, slot)
        all_keys = jnp.concatenate([keys, fresh_tokens[slot, :, :, 0]], 0)
        query_rows = queries[slot * NEW_TOKEN_COUNT : (slot + 1) * NEW_TOKEN_COUNT].reshape(
            NEW_TOKEN_COUNT, kv_local, query_group, HEAD_SIZE
        )
        scores = jnp.einsum(
            "ihgd,jhd->hgij", query_rows, all_keys, preferred_element_type=jnp.float32
        ) * HEAD_SIZE ** (-0.5)
        valid = jnp.arange(token_span, dtype=jnp.int32) < lengths[slot]
        allowed = jnp.concatenate(
            [jnp.broadcast_to(valid[None, :], (NEW_TOKEN_COUNT, token_span)), causal], 1
        )
        scores = jnp.where(allowed, scores, -jnp.inf)
        rowmax = jnp.max(scores, axis=-1, keepdims=True)
        expo = jnp.exp(scores - rowmax)
        probs = expo.astype(jnp.bfloat16)
        denom = jnp.sum(expo, axis=-1)
        values = arrange(values_in, slot)
        all_values = jnp.concatenate([values, fresh_tokens[slot, :, :, 1]], 0)
        mixed = jnp.einsum("hgij,jhd->ihgd", probs, all_values, preferred_element_type=jnp.float32)
        mixed = mixed / jnp.transpose(denom, (2, 0, 1))[..., None]
        outputs.append(mixed.reshape(NEW_TOKEN_COUNT, q_local * HEAD_SIZE).astype(jnp.bfloat16))
    attn = jnp.concatenate(outputs, 0)
    mine = lax.psum_scatter(
        jnp.dot(attn, o_weight, preferred_element_type=jnp.float32).astype(jnp.bfloat16),
        "tp",
        scatter_dimension=0,
        tiled=True,
    ).astype(jnp.float32)
    return (mine + residual.astype(jnp.float32)).astype(jnp.bfloat16)


def solution(mesh):
    placed = (
        P("pool", "tp"),
        P("pool", "tp"),
        P("pool", None, "tp"),
        P("tp", None),
        P(("pool", "tp"), None),
        P(),
        P(),
        P(),
    )
    return jax.shard_map(
        shards, mesh=mesh, in_specs=placed, out_specs=P(("pool", "tp"), None), check_vma=False
    )
```

profile of v0, /device:TPU:0, one launch (start us, length us, event | category | flops | bytes accessed | tf_op | source)
XLA Modules:
  0.0 688.6 jit_solution(6692819719967226467)
XLA Ops:
  8.4 11.8 %gather_fusion = bf16[32,256,1024]{2,1,0:T(8,128)(2,1)} fusion(bf16[24,256,1024]{2,1,0:T(8,128)(2,1)} %param.12, s32[1024]{0:T(1024)S(1)} %pad_clamp_fusion.2), kind=kCustom, calls=%fused_computation.4 | custom fusion | bytes 33554560 | tf_op jit(solution)/shard_map/jit(_take)/gather | solution.py:29
  20.2 22.5 %copy.65 = bf16[32,256,1024]{1,2,0:T(8,128)(2,1)} copy(bf16[32,256,1024]{2,1,0:T(8,128)(2,1)} %gather_fusion) | data formatting | bytes 33554432 | tf_op jit(solution)/shard_map/jit(_take)/gather | solution.py:29
  42.8 8.7 %select_select_fusion = bf16[16,2,256,4,2,128]{2,5,4,3,1,0:T(8,128)(2,1)S(1)} fusion(bf16[16,2,256,4,2,128]{2,5,4,3,1,0:T(8,128)(2,1)} %bitcast.104, pred[16,2]{1,0:T(8,128)(4,1)S(1)} %compare_and_fusion, pred[16,2]{1,0:T(8,128)(4,1)S(1)} %broadcast_in_dim.68), kind=kLoop, calls=%fused_computation.19 | loop fusion | flops 16777216 | bytes 33554496 | tf_op jit(solution)/shard_map/jit(_where)/select_n | solution.py:30
  51.4 6.2 fusion.45
  57.7 7.5 %all-to-all-start.1 = ((bf16[16,2,256,512]{2,3,1,0:T(8,128)(2,1)}), bf16[16,2,256,512]{2,3,1,0:T(8,128)(2,1)}, u32[]{:S(2)}, u32[]{:S(2)}) async-start(bf16[16,2,256,512]{2,3,1,0:T(8,128)(2,1)} %bitcast.106), calls=%async_computation.1 | async-start | bytes 16777216 | tf_op jit(solution)/shard_map/all_to_all | solution.py:53
  65.2 12.4 %copy.66 = bf16[16,2,256,512]{3,2,1,0:T(8,128)(2,1)} copy(bf16[16,2,256,512]{2,3,1,0:T(8,128)(2,1)} %bitcast.105) | data formatting | bytes 16777216 | tf_op jit(solution)/shard_map/reshape;squeeze | solution.py:35
  77.5 138.3 %all-to-all-done.1 = bf16[16,2,256,512]{2,3,1,0:T(8,128)(2,1)} async-done(((bf16[16,2,256,512]{2,3,1,0:T(8,128)(2,1)}), bf16[16,2,256,512]{2,3,1,0:T(8,128)(2,1)}, u32[]{:S(2)}, u32[]{:S(2)}) %all-to-all-start.1) | async-done | bytes 8388640 | tf_op jit(solution)/shard_map/all_to_all | solution.py:53
  215.9 36.5 %all-to-all-start = ((bf16[16,2,256,512]{3,2,1,0:T(8,128)(2,1)}), bf16[16,2,256,512]{3,2,1,0:T(8,128)(2,1)}, u32[]{:S(2)}, u32[]{:S(2)}) async-start(bf16[16,2,256,512]{3,2,1,0:T(8,128)(2,1)} %copy.66), calls=%async_computation | async-start | bytes 16777216 | tf_op jit(solution)/shard_map/all_to_all | solution.py:54
  261.5 5.8 slice_bitcast_fusion.2
  267.3 4.9 gather_fusion.2
  279.2 7.4 %reshape.95 = bf16[4096,4,128]{0,2,1:T(8,128)(2,1)} reshape(bf16[16,256,512]{1,0,2:T(8,128)(2,1)} %copy.70) | data formatting | bytes 8388608 | tf_op jit(solution)/shard_map/reshape | solution.py:49
  286.6 6.3 copy.72
  293.0 110.2 %all-to-all-done = bf16[16,2,256,512]{3,2,1,0:T(8,128)(2,1)} async-done(((bf16[16,2,256,512]{3,2,1,0:T(8,128)(2,1)}), bf16[16,2,256,512]{3,2,1,0:T(8,128)(2,1)}, u32[]{:S(2)}, u32[]{:S(2)}) %all-to-all-start) | async-done | bytes 8388640 | tf_op jit(solution)/shard_map/all_to_all | solution.py:54
  403.1 5.8 slice_bitcast_fusion.3
  408.9 5.0 gather_fusion.1
  418.5 6.9 %reshape.158 = bf16[4096,4,128]{2,1,0:T(4,128)(2,1)} reshape(bf16[16,256,512]{2,1,0:T(8,128)(2,1)} %broadcast_select_fusion.3) | data formatting | bytes 8388608 | tf_op jit(solution)/shard_map/reshape | solution.py:49
  425.4 7.6 %copy.93 = bf16[4096,4,128]{0,2,1:T(8,128)(2,1)} copy(bf16[4096,4,128]{2,1,0:T(4,128)(2,1)} %reshape.158) | data formatting | bytes 8388608 | tf_op jit(solution)/shard_map/reshape | solution.py:49
  433.0 4.9 gather_fusion.3
  437.9 5.0 gather_fusion.4
  450.1 6.9 %reshape.159 = bf16[4096,4,128]{2,1,0:T(4,128)(2,1)} reshape(bf16[16,256,512]{2,1,0:T(8,128)(2,1)} %broadcast_select_fusion.1) | data formatting | bytes 8388608 | tf_op jit(solution)/shard_map/reshape | solution.py:49
  457.0 7.6 %copy.94 = bf16[4096,4,128]{0,2,1:T(8,128)(2,1)} copy(bf16[4096,4,128]{2,1,0:T(4,128)(2,1)} %reshape.159) | data formatting | bytes 8388608 | tf_op jit(solution)/shard_map/reshape | solution.py:49
  464.6 6.5 copy.79
  471.1 7.4 %reshape.98 = bf16[4096,4,128]{0,2,1:T(8,128)(2,1)} reshape(bf16[16,256,512]{1,0,2:T(8,128)(2,1)} %copy.79) | data formatting | bytes 8388608 | tf_op jit(solution)/shard_map/reshape | solution.py:49
  478.5 6.3 copy.81
  484.8 15.7 %fusion.5 = (f32[4,4,128]{2,1,0:T(4,128)S(1)}, f32[4,4224,128,4]{2,1,3,0:T(8,128)}) fusion(pred[128,4224]{0,1:T(8,128)(4,1)S(1)} %get-tuple-element.23, bf16[128,4,4,128]{0,3,2,1:T(8,128)(2,1)S(1)} %bitcast.110, bf16[128,4,128]{2,0,1:T(8,128)(2,1)S(1)} %get-tuple-element.34, bf16[4096,4,128]{2,0,1:T(8,128)(2,1)} %copy.81), kind=kOutput, calls=%fused_computation.14 | convolution fusion | flops 2249193472 | bytes 40001536 | tf_op jit(solution)/shard_map/ihgd,jhd->hgij/dot_general | solution.py:62
  500.5 14.7 %fusion.2 = f32[4,4,128]{2,1,0:T(4,128)S(1)} fusion(f32[4,4224,128,4]{2,1,3,0:T(8,128)} %get-tuple-element.27, f32[4,4,128]{2,1,0:T(4,128)S(1)} %get-tuple-element.26, pred[128,4224]{0,1:T(8,128)(4,1)S(1)} %get-tuple-element.23), kind=kLoop, calls=%fused_computation.11 | loop fusion | flops 34600960 | bytes 35160064 | tf_op jit(solution)/shard_map/reduce_sum | solution.py:73
  515.2 13.3 %fusion.4 = (f32[4,4,128]{2,1,0:T(4,128)S(1)}, f32[4,4224,128,4]{2,1,3,0:T(8,128)}) fusion(pred[128,4224]{0,1:T(8,128)(4,1)S(1)} %get-tuple-element.22, bf16[128,4,4,128]{0,3,2,1:T(8,128)(2,1)S(1)} %bitcast.109, bf16[128,4,128]{2,0,1:T(8,128)(2,1)S(1)} %get-tuple-element.35, bf16[4096,4,128]{2,0,1:T(8,128)(2,1)S(1)} %copy-done.1), kind=kOutput, calls=%fused_computation.13 | convolution fusion | flops 2249193472 | bytes 40001536 | tf_op jit(solution)/shard_map/ihgd,jhd->hgij/dot_general | solution.py:62
  528.5 14.4 %fusion = f32[4,4,128]{2,1,0:T(4,128)S(1)} fusion(f32[4,4224,128,4]{2,1,3,0:T(8,128)} %get-tuple-element.29, f32[4,4,128]{2,1,0:T(4,128)S(1)} %get-tuple-element.28, pred[128,4224]{0,1:T(8,128)(4,1)S(1)} %get-tuple-element.22), kind=kLoop, calls=%fused_computation.9 | loop fusion | flops 34600960 | bytes 35160064 | tf_op jit(solution)/shard_map/reduce_sum | solution.py:73
  543.0 16.1 %divide_convert_fusion = bf16[128,4,4,128]{0,3,2,1:T(8,128)(2,1)S(1)} fusion(f32[4,4224,128,4]{2,1,3,0:T(8,128)} %get-tuple-element.27, f32[4,4,128]{2,1,0:T(4,128)S(1)} %get-tuple-element.26, pred[128,4224]{0,1:T(8,128)(4,1)S(1)} %get-tuple-element.23, bf16[128,4,128]{0,2,1:T(8,128)(2,1)S(1)} %bitcast.112, bf16[4096,4,128]{0,2,1:T(8,128)(2,1)} %copy.94, ...), kind=kOutput, calls=%fused_computation.51 | convolution fusion | flops 2258370560 | bytes 40009728 | tf_op jit(solution)/shard_map/hgij,jhd->ihgd/dot_general | solution.py:76
  559.1 16.3 %divide_convert_fusion.1 = bf16[128,4,4,128]{0,3,2,1:T(8,128)(2,1)S(1)} fusion(f32[4,4224,128,4]{2,1,3,0:T(8,128)} %get-tuple-element.29, f32[4,4,128]{2,1,0:T(4,128)S(1)} %get-tuple-element.28, pred[128,4224]{0,1:T(8,128)(4,1)S(1)} %get-tuple-element.22, bf16[128,4,128]{0,2,1:T(8,128)(2,1)S(1)} %bitcast.111, bf16[4096,4,128]{0,2,1:T(8,128)(2,1)} %copy.93, ...), kind=kOutput, calls=%fused_computation.52 | convolution fusion | flops 2258370560 | bytes 40009728 | tf_op jit(solution)/shard_map/hgij,jhd->ihgd/dot_general | solution.py:76
  575.4 16.6 %convolution_convert_fusion = bf16[256,8192]{1,0:T(8,128)(2,1)} fusion(bf16[2048,8192]{1,0:T(8,128)(2,1)} %param.13, bf16[128,2048]{0,1:T(8,128)(2,1)S(1)} %bitcast.107, bf16[128,2048]{0,1:T(8,128)(2,1)S(1)} %bitcast.108), kind=kOutput, calls=%fused_computation.20 | convolution fusion | flops 8594128896 | bytes 38797312 | tf_op jit(solution)/shard_map/dot_general | solution.py:81
  592.1 86.3 %reduce-scatter.2.cloned.1.call-done = bf16[128,8192]{1,0:T(8,128)(2,1)} async-done(((bf16[256,8192]{1,0:T(8,128)(2,1)}), bf16[128,8192]{1,0:T(8,128)(2,1)}) %reduce-scatter.2.cloned.1.call-update) | async-done | bytes 2097168 | tf_op jit(solution)/shard_map/reduce_scatter | solution.py:80
  (53 shorter events, 33.0 us)
Async XLA Ops:
  57.7 158.2 %all-to-all-start.1 = ((bf16[16,2,256,512]{2,3,1,0:T(8,128)(2,1)}), bf16[16,2,256,512]{2,3,1,0:T(8,128)(2,1)}, u32[]{:S(2)}, u32[]{:S(2)}) async-start(bf16[16,2,256,512]{2,3,1,0:T(8,128)(2,1)} %bitcast.106), calls=%async_computation.1 | async-start | bytes 16777216 | tf_op jit(solution)/shard_map/all_to_all | solution.py:53
  77.5 175.0 %copy-start.6 = (s32[32]{0:T(128)S(1)}, s32[32]{0:T(128)}, u32[]{:S(2)}) copy-start(s32[32]{0:T(128)} %param.17) | copy-start | bytes 388
  77.5 177.0 %copy-start.4 = (bf16[256,1024]{1,0:T(8,128)(2,1)S(1)}, bf16[256,1024]{1,0:T(8,128)(2,1)}, u32[]{:S(2)}) copy-start(bf16[256,1024]{1,0:T(8,128)(2,1)} %param.11) | copy-start | bytes 1572868
  77.5 178.4 %copy-start.3 = (bf16[256,2048]{1,0:T(8,128)(2,1)S(1)}, bf16[256,2048]{1,0:T(8,128)(2,1)}, u32[]{:S(2)}) copy-start(bf16[256,2048]{1,0:T(8,128)(2,1)} %param.10) | copy-start | bytes 3145732
  77.5 179.1 %copy-start.5 = (s32[32,16]{0,1:T(8,128)S(1)}, s32[32,16]{0,1:T(8,128)}, u32[]{:S(2)}) copy-start(s32[32,16]{0,1:T(8,128)} %param.15) | copy-start | bytes 6148
  215.9 187.3 %all-to-all-start = ((bf16[16,2,256,512]{3,2,1,0:T(8,128)(2,1)}), bf16[16,2,256,512]{3,2,1,0:T(8,128)(2,1)}, u32[]{:S(2)}, u32[]{:S(2)}) async-start(bf16[16,2,256,512]{3,2,1,0:T(8,128)(2,1)} %copy.66), calls=%async_computation | async-start | bytes 16777216 | tf_op jit(solution)/shard_map/all_to_all | solution.py:54
  252.4 425.9 %reduce-scatter.2.cloned.1.call-start = ((), (), s32[]{:S(2)}) async-start(), calls=%async_computation.3 | async-start | bytes 6291456 | tf_op jit(solution)/shard_map/reduce_scatter | solution.py:80
  442.9 4.8 copy-start
  500.5 14.7 %copy-start.1 = (bf16[4096,4,128]{2,0,1:T(8,128)(2,1)S(1)}, bf16[4096,4,128]{2,0,1:T(8,128)(2,1)}, u32[]{:S(2)}) copy-start(bf16[4096,4,128]{2,0,1:T(8,128)(2,1)} %copy.72) | copy-start | bytes 12582916
  575.4 102.9 %copy-start.2 = (bf16[128,8192]{1,0:T(8,128)(2,1)S(1)}, bf16[128,8192]{1,0:T(8,128)(2,1)}, u32[]{:S(2)}) copy-start(bf16[128,8192]{1,0:T(8,128)(2,1)} %param.14) | copy-start | bytes 6291460
Sparse Core Ops, SparseCore 0:
  592.2 86.0 reduce-scatter.1
where the time goes:
time: 692 us; the launch traced here: 689 us
  waiting for transfers between devices  335 us (48%)
  local copies, waits for them, and re-layouts  155 us (22%)
  matrix products  78.1 us (11%)
  other arithmetic  63 us (9%)
  starting transfers between devices  44.1 us (6%)
  between operations  13.7 us (2%)
    all_to_all x1, waiting for transfers between devices, shards(): lax.all_to_all(own_keys, 'pool', split_axis=0, concat_axis=0, tiled=True)  138 us
    all_to_all x1, waiting for transfers between devices, shards(): lax.all_to_all(own_values, 'pool', split_axis=0, concat_axis=0, tiled=True)  110 us
    reduce_scatter x1, waiting for transfers between devices, shards(): lax.psum_scatter(jnp.dot(attn, o_weight, preferred_element_type=jnp.float...  86.3 us
    reshape x8, local copies, waits for them, and re-layouts, arrange(): return ordered.reshape(token_span, kv_local, HEAD_SIZE)  56.4 us
    all_to_all x1, starting transfers between devices, shards(): lax.all_to_all(own_values, 'pool', split_axis=0, concat_axis=0, tiled=True)  36.5 us
    gather x2, local copies, waits for them, and re-layouts, shards(): outgoing = jnp.take(key_value_store, chosen, axis=0)  34.3 us
    dot_general x2, matrix products, shards(): jnp.einsum('hgij,jhd->ihgd', probs, all_values, preferred_element_type=jn...  32.4 us
    reduce_sum x2, other arithmetic, shards(): denom = jnp.sum(expo, axis=-1)  29.1 us
  transfers between devices with their start and end apart: 3, of which 3 were waited for; matrix products, arithmetic and copies ran while one was open for 8% of the time, Pallas kernels for 0%

commit v1 on v0

v1 whole, which is shorter than its diff:
```python
import functools

import jax
import jax.numpy as jnp
from jax import lax
from jax.experimental import pallas as pl
from jax.experimental.pallas import tpu as pltpu
from jax.sharding import PartitionSpec as P

HEAD_SIZE = 128
NEW_TOKEN_COUNT = 128
PREFIX_BLOCK_LEN = 256
MAXB = 16
LOG2E = 1.4426950408889634
SCALE2 = HEAD_SIZE ** (-0.5) * LOG2E
NEG = -1e30
F32 = jnp.float32
BF16 = jnp.bfloat16
TOK = NEW_TOKEN_COUNT
STAT = 128


def dot_nt(a, b):
    return lax.dot_general(a, b, (((1,), (1,)), ((), ())), preferred_element_type=F32)


def chip_ring(nchips):
    if nchips % 2:
        return list(range(nchips))
    up = list(range(0, nchips, 2))
    return up + [chip + 1 for chip in reversed(up)]


def pack_kernel(idx_ref, src_ref, dst_ref):
    dst_ref[...] = src_ref[...]


def pack_blocks(indices, store):
    count = indices.shape[0]
    _, rows, cols = store.shape
    return pl.pallas_call(
        pack_kernel,
        out_shape=jax.ShapeDtypeStruct((count, rows, cols), store.dtype),
        grid_spec=pltpu.PrefetchScalarGridSpec(
            num_scalar_prefetch=1,
            grid=(count,),
            in_specs=[pl.BlockSpec((1, rows, cols), lambda i, idx: (idx[i], 0, 0))],
            out_specs=pl.BlockSpec((1, rows, cols), lambda i, idx: (i, 0, 0)),
        ),
        cost_estimate=pl.CostEstimate(
            flops=0, bytes_accessed=4 * count * rows * cols, transcendentals=0
        ),
        name="pack_blocks",
    )(indices, store)


def attend_kernel(call, group, heads, has_carry, has_fresh, plan_ref, *refs):
    refs = list(refs)
    q_ref, own_ref, sib_ref = refs[:3]
    rest = refs[3:]
    fresh_ref = rest.pop(0) if has_fresh else None
    carry_ref = rest.pop(0) if has_carry else None
    out_ref = rest.pop(0)
    h = pl.program_id(0)
    width = group * HEAD_SIZE
    rows = group * TOK
    n_own = plan_ref[4 * call + 2]
    n_sib = plan_ref[4 * call + 3]

    q = jnp.concatenate(
        [q_ref[:, g * HEAD_SIZE : (g + 1) * HEAD_SIZE] for g in range(group)], axis=0
    )
    parts = [own_ref[0], sib_ref[0]]
    if has_fresh:
        parts.append(fresh_ref[...])
    keys = jnp.concatenate([x[:, :HEAD_SIZE] for x in parts], axis=0)
    values = jnp.concatenate([x[:, HEAD_SIZE:] for x in parts], axis=0)
    span = keys.shape[0]
    values = jnp.concatenate([values, jnp.ones((span, HEAD_SIZE), BF16)], axis=1)
    scores = dot_nt(q, keys)
    col = lax.broadcasted_iota(jnp.int32, (1, 2 * PREFIX_BLOCK_LEN), 1)
    limit = jnp.where(col < PREFIX_BLOCK_LEN, n_own, n_sib + PREFIX_BLOCK_LEN)
    bias = jnp.where(col < limit, 0.0, NEG).astype(F32)
    if has_fresh:
        tok = lax.broadcasted_iota(jnp.int32, (TOK, TOK), 0)
        new = lax.broadcasted_iota(jnp.int32, (TOK, TOK), 1)
        causal = jnp.where(new <= tok, 0.0, NEG).astype(F32)
        causal = jnp.concatenate([causal] * group, axis=0)
        scores = jnp.concatenate(
            [
                scores[:, : 2 * PREFIX_BLOCK_LEN] + bias,
                scores[:, 2 * PREFIX_BLOCK_LEN :] + causal,
            ],
            axis=1,
        )
    else:
        scores = scores + bias
    top = jnp.max(scores, axis=1, keepdims=True)
    probs = jnp.exp2((scores - top) * SCALE2).astype(BF16)
    mixed = jnp.dot(probs, values, preferred_element_type=F32)
    total = mixed[:, HEAD_SIZE:]
    out = mixed[:, :HEAD_SIZE] / total
    lse = top * SCALE2 + jnp.log2(total)

    lane = lax.broadcasted_iota(jnp.int32, (TOK, STAT), 1)
    stat_at = heads * HEAD_SIZE
    if has_carry:
        stat_in = carry_ref[:, stat_at : stat_at + STAT].astype(F32)
    old = out_ref[:, stat_at : stat_at + STAT].astype(F32)
    stat = jnp.where(h == 0, 0.0, old)
    pieces = []
    for g in range(group):
        head = h * group + g
        o_g = out[g * TOK : (g + 1) * TOK]
        lse_g = lse[g * TOK : (g + 1) * TOK]
        if has_carry:
            mine = (lax.rem(lane, heads) == head) & (lane < 3 * heads)
            lse_c = jnp.sum(jnp.where(mine, stat_in, 0.0), axis=1, keepdims=True)
            at = pl.multiple_of(head * HEAD_SIZE, HEAD_SIZE)
            o_c = carry_ref[:, pl.ds(at, HEAD_SIZE)].astype(F32)
            high = jnp.maximum(lse_g, lse_c)
            w_c = jnp.exp2(lse_c - high)
            w_g = jnp.exp2(lse_g - high)
            w = w_c + w_g
            o_g = (o_c * w_c + o_g * w_g) / w
            lse_g = high + jnp.log2(w)
        first = lse_g.astype(BF16).astype(F32)
        second = (lse_g - first).astype(BF16).astype(F32)
        third = lse_g - first - second
        stat = jnp.where(lane == head, first, stat)
        stat = jnp.where(lane == head + heads, second, stat)
        stat = jnp.where(lane == head + 2 * heads, third, stat)
        pieces.append(o_g.astype(BF16))
    at = pl.multiple_of(h * width, width)
    out_ref[:, pl.ds(at, width)] = jnp.concatenate(pieces, axis=1)
    out_ref[:, stat_at : stat_at + STAT] = stat.astype(BF16)


def attend(call, plan, q, store, sib, kv_local, fresh=None, carry=None):
    heads = q.shape[1] // HEAD_SIZE
    group = heads // kv_local
    width = group * HEAD_SIZE
    pair = 2 * HEAD_SIZE
    cols = heads * HEAD_SIZE + STAT
    span = 2 * PREFIX_BLOCK_LEN + (TOK if fresh is not None else 0)
    in_specs = [
        pl.BlockSpec((TOK, width), lambda h, plan: (0, h)),
        pl.BlockSpec((1, PREFIX_BLOCK_LEN, pair), lambda h, plan: (plan[4 * call], 0, h)),
        pl.BlockSpec((1, PREFIX_BLOCK_LEN, pair), lambda h, plan: (plan[4 * call + 1], 0, h)),
    ]
    args = [q, store, sib]
    if fresh is not None:
        in_specs.append(pl.BlockSpec((TOK, pair), lambda h, plan: (0, h)))
        args.append(fresh)
    if carry is not None:
        in_specs.append(pl.BlockSpec((TOK, cols), lambda h, plan: (0, 0)))
        args.append(carry)
    body = functools.partial(
        attend_kernel, call, group, heads, carry is not None, fresh is not None
    )
    return pl.pallas_call(
        body,
        out_shape=jax.ShapeDtypeStruct((TOK, cols), BF16),
        grid_spec=pltpu.PrefetchScalarGridSpec(
            num_scalar_prefetch=1,
            grid=(kv_local,),
            in_specs=in_specs,
            out_specs=pl.BlockSpec((TOK, cols), lambda h, plan: (0, 0)),
        ),
        compiler_params=pltpu.CompilerParams(vmem_limit_bytes=40 * 1024 * 1024),
        cost_estimate=pl.CostEstimate(
            flops=8 * heads * TOK * span * HEAD_SIZE,
            bytes_accessed=4 * TOK * cols + 4 * kv_local * span * pair,
            transcendentals=heads * TOK * span,
        ),
        name="attend",
    )(plan, *args)


def merge_parts(heads, part_refs, attn_ref):
    stat_at = heads * HEAD_SIZE
    stats = [ref[:, stat_at : stat_at + STAT].astype(F32) for ref in part_refs]
    for head in range(heads):
        lses = [
            s[:, head : head + 1]
            + s[:, head + heads : head + heads + 1]
            + s[:, head + 2 * heads : head + 2 * heads + 1]
            for s in stats
        ]
        high = functools.reduce(jnp.maximum, lses)
        weights = [jnp.exp2(x - high) for x in lses]
        norm = 1.0 / functools.reduce(jnp.add, weights)
        cols = slice(head * HEAD_SIZE, (head + 1) * HEAD_SIZE)
        mixed = functools.reduce(
            jnp.add, [w * ref[:, cols].astype(F32) for w, ref in zip(weights, part_refs)]
        )
        attn_ref[:, cols] = (mixed * norm).astype(BF16)


def project_kernel(heads, nparts, nadd, *refs):
    part_refs = refs[:nparts]
    w_ref = refs[nparts]
    add_refs = refs[nparts + 1 : nparts + 1 + nadd]
    out_ref, attn_ref = refs[nparts + 1 + nadd :]

    @pl.when(pl.program_id(0) == 0)
    def _():
        merge_parts(heads, part_refs, attn_ref)

    got = jnp.dot(attn_ref[...], w_ref[...], preferred_element_type=F32).astype(BF16)
    if nadd:
        total = got.astype(F32)
        for ref in add_refs:
            total = total + ref[...].astype(F32)
        got = total.astype(BF16)
    out_ref[...] = got


def project(parts, weight, adds=()):
    depth, model = weight.shape
    heads = depth // HEAD_SIZE
    cols = parts[0].shape[1]
    tile = 512
    in_specs = [pl.BlockSpec((TOK, cols), lambda j: (0, 0)) for _ in parts]
    in_specs.append(pl.BlockSpec((depth, tile), lambda j: (0, j)))
    in_specs += [pl.BlockSpec((TOK, tile), lambda j: (0, j)) for _ in adds]
    return pl.pallas_call(
        functools.partial(project_kernel, heads, len(parts), len(adds)),
        out_shape=jax.ShapeDtypeStruct((TOK, model), BF16),
        grid=(model // tile,),
        in_specs=in_specs,
        out_specs=pl.BlockSpec((TOK, tile), lambda j: (0, j)),
        scratch_shapes=[pltpu.VMEM((TOK, depth), BF16)],
        compiler_params=pltpu.CompilerParams(vmem_limit_bytes=40 * 1024 * 1024),
        cost_estimate=pl.CostEstimate(
            flops=2 * TOK * depth * model,
            bytes_accessed=2 * depth * model + 4 * TOK * model,
            transcendentals=0,
        ),
        name="project",
    )(*parts, weight, *adds)


def shards(
    queries, new_key_values, key_value_store, o_weight, residual, hit_dev, hit_blk, prefix_len
):
    npool = lax.axis_size("pool")
    ntp = lax.axis_size("tp")
    me = lax.axis_index("pool")
    tp = lax.axis_index("tp")
    rdev = queries.shape[0] // TOK
    kv_local = key_value_store.shape[2] // (2 * HEAD_SIZE)
    nchips = npool // 2
    core = lax.rem(me, 2)
    chip = lax.div(me, 2)
    sibling = me + 1 - 2 * core
    ring = chip_ring(nchips)
    place = [ring.index(i) for i in range(nchips)]
    split_rows = ntp == rdev and rdev == 2

    swap_perm = [(p, p + 1 - 2 * (p % 2)) for p in range(npool)]
    cw_perm, ccw_perm = [], []
    for k in range(nchips):
        a, b = ring[k], ring[(k + 1) % nchips]
        for c in range(2):
            cw_perm.append((2 * a + c, 2 * b + c))
            ccw_perm.append((2 * b + c, 2 * a + c))

    starts = jnp.arange(MAXB, dtype=jnp.int32)[None, :] * PREFIX_BLOCK_LEN
    left = jnp.clip(prefix_len[:, None] - starts, 0, PREFIX_BLOCK_LEN)
    here = hit_dev == me
    n_own = jnp.sum(jnp.where(here, left, 0), axis=1)
    blk_own = jnp.sum(jnp.where(here, hit_blk, 0), axis=1)
    n_sib = jnp.sum(jnp.where(hit_dev == sibling, left, 0), axis=1)

    def of_core(x, which):
        x = x.reshape(nchips, 2, rdev)
        return lax.dynamic_index_in_dim(x, which, 1, keepdims=False)

    blk_mine, blk_theirs = of_core(blk_own, core), of_core(blk_own, 1 - core)
    n_own, n_sib = of_core(n_own, core), of_core(n_sib, core)
    spot = jnp.asarray(place, jnp.int32)[chip]
    ring_at = jnp.asarray(ring, jnp.int32)
    steps = list(range(-(nchips // 2), nchips // 2 + 1))
    chips_at = ring_at[lax.rem(spot + nchips - jnp.asarray(steps, jnp.int32), nchips)]

    half = nchips // 2
    outs = []
    slots = [1 - tp, tp] if split_rows else list(range(rdev))
    state = []
    for order, slot in enumerate(slots):
        pick = lambda x: lax.dynamic_index_in_dim(x, slot, 1, keepdims=False)
        plan = jnp.stack(
            [pick(blk_mine)[chips_at], chips_at, pick(n_own)[chips_at], pick(n_sib)[chips_at]],
            axis=1,
        ).reshape(-1)
        q = lax.dynamic_slice_in_dim(queries, slot * TOK, TOK, 0)
        fresh = lax.dynamic_slice_in_dim(new_key_values, slot * TOK, TOK, 0)
        packed = pack_blocks(pick(blk_theirs), key_value_store)
        sib = lax.ppermute(packed, "pool", swap_perm)
        if nchips % 2:
            reach = (half, half)
        else:
            reach = (half, half - 1) if order % 2 == 0 else (half - 1, half)
        held = {}
        for sign, perm, hops in ((1, cw_perm, reach[0]), (-1, ccw_perm, reach[1])):
            moving = q
            for s in range(1, hops + 1):
                moving = lax.ppermute(moving, "pool", perm)
                held[sign * s] = moving
        state.append((plan, q, fresh, sib, reach, held))

    parts_of = []
    for plan, q, fresh, sib, reach, held in state:
        run = functools.partial(attend, store=key_value_store, sib=sib, kv_local=kv_local)
        call = lambda s: steps.index(s)
        own = run(call(0), plan, q, fresh=fresh)
        parts = [own]
        for sign, back, hops in ((1, ccw_perm, reach[0]), (-1, cw_perm, reach[1])):
            carry = None
            for s in range(hops, 0, -1):
                carry = run(call(sign * s), plan, held[sign * s], carry=carry)
                carry = lax.ppermute(carry, "pool", back)
            if carry is not None:
                parts.append(carry)
        parts_of.append(parts)

    if split_rows:
        away = project(parts_of[0], o_weight)
        got = lax.ppermute(away, "tp", [(0, 1), (1, 0)])
        return project(parts_of[1], o_weight, (got, residual))
    rows = jnp.concatenate([project(parts, o_weight) for parts in parts_of], axis=0)
    mine = lax.psum_scatter(rows, "tp", scatter_dimension=0, tiled=True)
    return (mine.astype(F32) + residual.astype(F32)).astype(BF16)


def solution(mesh):
    placed = (
        P("pool", "tp"),
        P("pool", "tp"),
        P("pool", None, "tp"),
        P("tp", None),
        P(("pool", "tp"), None),
        P(),
        P(),
        P(),
    )
    return jax.shard_map(
        shards, mesh=mesh, in_specs=placed, out_specs=P(("pool", "tp"), None), check_vma=False
    )
```

time: 692 us -> 258 us (0.37)
  waiting for transfers between devices: 335 us -> 67.7 us
  local copies, waits for them, and re-layouts: 155 us -> 8.89 us
  Pallas kernels: 0 us -> 141 us
  matrix products: 78.1 us -> 0 us
  other arithmetic: 63 us -> 0.87 us
  between operations: 13.7 us -> 1 us
  starting transfers between devices: 44.1 us -> 36.5 us
    all_to_all x2 -> x0, waiting for transfers between devices: 249 us -> none  [the longest x1 138 us: shards(): lax.all_to_all(own_keys, 'pool', split_axis=0, concat_axis=0, tiled=True)]
    pallas_call x0 -> x20, Pallas kernels: none -> 141 us  [the longest x16 86.4 us: attend(): pl.pallas_call(body, out_shape=jax.ShapeDtypeStruct((TOK, cols), BF16), g...]
    reduce_scatter x1 -> x0, waiting for transfers between devices: 86.3 us -> none  [shards(): lax.psum_scatter(jnp.dot(attn, o_weight, preferred_element_type=jnp.float...]
    dot_general x5 -> x0, matrix products: 78.1 us -> none  [the longest x2 32.4 us: shards(): jnp.einsum('hgij,jhd->ihgd', probs, all_values, preferred_element_type=jn...]
    ppermute x0 -> x31, waiting for transfers between devices: none -> 67.7 us  [the longest x14 46.9 us: shards(): moving = lax.ppermute(moving, 'pool', perm)]
    reshape x9 -> x5, local copies, waits for them, and re-layouts: 56.7 us -> 0.43 us  [the longest x3 0.27 us: of_core(): x = x.reshape(nchips, 2, rdev)]
    gather x6 -> x7, local copies, waits for them, and re-layouts: 54.1 us -> 4.65 us  [the longest x2 1.33 us: shards(): pick(n_own)[chips_at]]
    all_to_all x2 -> x0, starting transfers between devices: 44 us -> none  [the longest x1 36.5 us: shards(): lax.all_to_all(own_values, 'pool', split_axis=0, concat_axis=0, tiled=True)]
  transfers between devices with their start and end apart: 3 -> 31, of which waited for: 3 -> 16; matrix products, arithmetic and copies ran while one was open for 8% -> 3% of each run, Pallas kernels for 0% -> 44%
where the time goes in v1:
time: 258 us; the launch traced here: 256 us
  Pallas kernels  141 us (55%)
  waiting for transfers between devices  67.7 us (26%)
  starting transfers between devices  36.5 us (14%)
  local copies, waits for them, and re-layouts  8.89 us (3%)
    pallas_call x16, Pallas kernels, attend(): pl.pallas_call(body, out_shape=jax.ShapeDtypeStruct((TOK, cols), BF16), g...  86.4 us
    ppermute x14, waiting for transfers between devices, shards(): moving = lax.ppermute(moving, 'pool', perm)  46.9 us
    pallas_call x2, Pallas kernels, project(): pl.pallas_call(functools.partial(project_kernel, heads, len(parts), len(a...  40.2 us
    ppermute x14, waiting for transfers between devices, shards(): carry = lax.ppermute(carry, 'pool', back)  20.8 us
    ppermute x14, starting transfers between devices, shards(): moving = lax.ppermute(moving, 'pool', perm)  17.1 us
    ppermute x14, starting transfers between devices, shards(): carry = lax.ppermute(carry, 'pool', back)  16.7 us
    pallas_call x2, Pallas kernels, pack_blocks(): pl.pallas_call(pack_kernel, out_shape=jax.ShapeDtypeStruct((count, rows,...  14.4 us
  transfers between devices with their start and end apart: 31, of which 16 were waited for; matrix products, arithmetic and copies ran while one was open for 3% of the time, Pallas kernels for 44%

profile of v1, /device:TPU:0, one launch (start us, length us, event | category | flops | bytes accessed | tf_op | source)
XLA Modules:
  0.0 255.9 jit_solution(9825137866362405784)
XLA Ops:
  2.4 7.0 %pack_blocks.3 = bf16[8,256,1024]{2,1,0:T(8,128)(2,1)} custom-call(s32[8]{0:T(128)} %get-tuple-element.5.idx_ref, bf16[24,256,1024]{2,1,0:T(8,128)(2,1)} %refs_1_.31), custom_call_target="tpu_custom_call" | custom-call | bytes 8388608 | tf_op jit(solution)/shard_map/pack_blocks/pallas_call | solution.py:41
  10.4 2.8 %collective-permute-start.16 = (bf16[128,2048]{1,0:T(8,128)(2,1)S(1)}, bf16[128,2048]{1,0:T(8,128)(2,1)S(1)}, u32[]{:S(2)}, u32[]{:S(2)}) collective-permute-start(bf16[128,2048]{1,0:T(8,128)(2,1)S(1)} %get-tuple-element.16.refs_0_), channel_id=1, source_target_pairs={{0,8},{2,10},{8,16},{10,18},{16,24},{18,26},{24,28},{26,30},{28,20... | collective-permute-start | bytes 1572872 | tf_op jit(solution)/shard_map/ppermute | solution.py:309
  13.2 7.4 %pack_blocks.2 = bf16[8,256,1024]{2,1,0:T(8,128)(2,1)} custom-call(s32[8]{0:T(128)} %get-tuple-element.7.idx_ref, bf16[24,256,1024]{2,1,0:T(8,128)(2,1)} %refs_1_.31), custom_call_target="tpu_custom_call" | custom-call | bytes 8388608 | tf_op jit(solution)/shard_map/pack_blocks/pallas_call | solution.py:41
  20.7 4.9 %collective-permute-done.16.refs_0_ = bf16[128,2048]{1,0:T(8,128)(2,1)S(1)} collective-permute-done((bf16[128,2048]{1,0:T(8,128)(2,1)S(1)}, bf16[128,2048]{1,0:T(8,128)(2,1)S(1)}, u32[]{:S(2)}, u32[]{:S(2)}) %collective-permute-start.16) | collective-permute-done | bytes 524320 | tf_op jit(solution)/shard_map/ppermute | solution.py:309
  27.6 11.7 %collective-permute-done.17.refs_0_ = bf16[128,2048]{1,0:T(8,128)(2,1)S(1)} collective-permute-done((bf16[128,2048]{1,0:T(8,128)(2,1)S(1)}, bf16[128,2048]{1,0:T(8,128)(2,1)S(1)}, u32[]{:S(2)}, u32[]{:S(2)}) %collective-permute-start.17) | collective-permute-done | bytes 524320 | tf_op jit(solution)/shard_map/ppermute | solution.py:309
  44.3 8.0 %collective-permute-done.18.refs_0_ = bf16[128,2048]{1,0:T(8,128)(2,1)} collective-permute-done((bf16[128,2048]{1,0:T(8,128)(2,1)S(1)}, bf16[128,2048]{1,0:T(8,128)(2,1)}, u32[]{:S(2)}, u32[]{:S(2)}) %collective-permute-start.18) | collective-permute-done | bytes 524320 | tf_op jit(solution)/shard_map/ppermute | solution.py:309
  58.6 5.9 %collective-permute-done.25.refs_0_ = bf16[128,2048]{1,0:T(8,128)(2,1)} collective-permute-done((bf16[128,2048]{1,0:T(8,128)(2,1)S(1)}, bf16[128,2048]{1,0:T(8,128)(2,1)}, u32[]{:S(2)}, u32[]{:S(2)}) %collective-permute-start.25) | collective-permute-done | bytes 524320 | tf_op jit(solution)/shard_map/ppermute | solution.py:309
  65.3 5.1 %attend.25 = bf16[128,2176]{1,0:T(8,128)(2,1)S(1)} custom-call(s32[36]{0:T(128)S(1)} %reshape.57.plan_ref, bf16[128,2048]{1,0:T(8,128)(2,1)} %collective-permute-done.19.refs_0_, bf16[24,256,1024]{2,1,0:T(8,128)(2,1)} %refs_1_.31, bf16[8,256,1024]{2,1,0:T(8,128)(2,1)} %collective-permute-done.15.refs_2_), custom_call_target="tpu_custom_call" | custom-call | flops 1073741824 | bytes 3211264 | tf_op jit(solution)/shard_map/attend/pallas_call | solution.py:161
  73.4 6.2 %collective-permute-done.26.refs_0_ = bf16[128,2048]{1,0:T(8,128)(2,1)S(1)} collective-permute-done((bf16[128,2048]{1,0:T(8,128)(2,1)}, bf16[128,2048]{1,0:T(8,128)(2,1)S(1)}, u32[]{:S(2)}, u32[]{:S(2)}) %collective-permute-start.26) | collective-permute-done | bytes 524320 | tf_op jit(solution)/shard_map/ppermute | solution.py:309
  79.6 5.0 %attend.29 = bf16[128,2176]{1,0:T(8,128)(2,1)S(1)} custom-call(s32[36]{0:T(128)S(1)} %reshape.57.plan_ref, bf16[128,2048]{1,0:T(8,128)(2,1)S(1)} %collective-permute-done.26.refs_0_, bf16[24,256,1024]{2,1,0:T(8,128)(2,1)} %refs_1_.31, bf16[8,256,1024]{2,1,0:T(8,128)(2,1)} %collective-permute-done.15.refs_2_), custom_call_target="tpu_custom_call" | custom-call | flops 1073741824 | bytes 3211264 | tf_op jit(solution)/shard_map/attend/pallas_call | solution.py:161
  86.4 5.1 %collective-permute-done.20.refs_3_ = bf16[128,2176]{1,0:T(8,128)(2,1)S(1)} collective-permute-done((bf16[128,2176]{1,0:T(8,128)(2,1)S(1)}, bf16[128,2176]{1,0:T(8,128)(2,1)S(1)}, u32[]{:S(2)}, u32[]{:S(2)}) %collective-permute-start.20) | collective-permute-done | bytes 557088 | tf_op jit(solution)/shard_map/ppermute | solution.py:323
  91.5 5.4 %attend.26 = bf16[128,2176]{1,0:T(8,128)(2,1)S(1)} custom-call(s32[36]{0:T(128)S(1)} %reshape.57.plan_ref, bf16[128,2048]{1,0:T(8,128)(2,1)} %collective-permute-done.18.refs_0_, bf16[24,256,1024]{2,1,0:T(8,128)(2,1)} %refs_1_.31, bf16[8,256,1024]{2,1,0:T(8,128)(2,1)} %collective-permute-done.15.refs_2_, bf16[128,2176]{1,0:T(8,128)(2,1)S(1)} %collective-permute-done.20.refs_3_), custom_call_target="tpu_custom_call" | custom-call | flops 1073741824 | bytes 3211264 | tf_op jit(solution)/shard_map/attend/pallas_call | solution.py:161
  99.0 3.7 %collective-permute-done.8.refs_0_ = bf16[128,2048]{1,0:T(8,128)(2,1)S(1)} collective-permute-done((bf16[128,2048]{1,0:T(8,128)(2,1)S(1)}, bf16[128,2048]{1,0:T(8,128)(2,1)S(1)}, u32[]{:S(2)}, u32[]{:S(2)}) %collective-permute-start.8) | collective-permute-done | bytes 524320 | tf_op jit(solution)/shard_map/ppermute | solution.py:309
  103.5 5.4 %attend.30 = bf16[128,2176]{1,0:T(8,128)(2,1)S(1)} custom-call(s32[36]{0:T(128)S(1)} %reshape.57.plan_ref, bf16[128,2048]{1,0:T(8,128)(2,1)} %collective-permute-done.25.refs_0_, bf16[24,256,1024]{2,1,0:T(8,128)(2,1)} %refs_1_.31, bf16[8,256,1024]{2,1,0:T(8,128)(2,1)} %collective-permute-done.15.refs_2_, bf16[128,2176]{1,0:T(8,128)(2,1)S(1)} %collective-permute-done.27.refs_3_), custom_call_target="tpu_custom_call" | custom-call | flops 1073741824 | bytes 3211264 | tf_op jit(solution)/shard_map/attend/pallas_call | solution.py:161
  110.3 4.4 %collective-permute-done.21.refs_3_ = bf16[128,2176]{1,0:T(8,128)(2,1)S(1)} collective-permute-done((bf16[128,2176]{1,0:T(8,128)(2,1)S(1)}, bf16[128,2176]{1,0:T(8,128)(2,1)S(1)}, u32[]{:S(2)}, u32[]{:S(2)}) %collective-permute-start.21) | collective-permute-done | bytes 557088 | tf_op jit(solution)/shard_map/ppermute | solution.py:323
  114.7 5.3 %attend.27 = bf16[128,2176]{1,0:T(8,128)(2,1)S(1)} custom-call(s32[36]{0:T(128)S(1)} %reshape.57.plan_ref, bf16[128,2048]{1,0:T(8,128)(2,1)S(1)} %collective-permute-done.17.refs_0_, bf16[24,256,1024]{2,1,0:T(8,128)(2,1)} %refs_1_.31, bf16[8,256,1024]{2,1,0:T(8,128)(2,1)} %collective-permute-done.15.refs_2_, ...), custom_call_target="tpu_custom_call" | custom-call | flops 1073741824 | bytes 3211264 | tf_op jit(solution)/shard_map/attend/pallas_call | solution.py:161
  122.1 3.9 %collective-permute-done.9.refs_0_ = bf16[128,2048]{1,0:T(8,128)(2,1)} collective-permute-done((bf16[128,2048]{1,0:T(8,128)(2,1)S(1)}, bf16[128,2048]{1,0:T(8,128)(2,1)}, u32[]{:S(2)}, u32[]{:S(2)}) %collective-permute-start.9) | collective-permute-done | bytes 524320 | tf_op jit(solution)/shard_map/ppermute | solution.py:309
  126.8 5.3 %attend.31 = bf16[128,2176]{1,0:T(8,128)(2,1)S(1)} custom-call(s32[36]{0:T(128)S(1)} %reshape.57.plan_ref, bf16[128,2048]{1,0:T(8,128)(2,1)S(1)} %collective-permute-done.24.refs_0_, bf16[24,256,1024]{2,1,0:T(8,128)(2,1)} %refs_1_.31, bf16[8,256,1024]{2,1,0:T(8,128)(2,1)} %collective-permute-done.15.refs_2_, ...), custom_call_target="tpu_custom_call" | custom-call | flops 1073741824 | bytes 3211264 | tf_op jit(solution)/shard_map/attend/pallas_call | solution.py:161
  133.4 4.4 %collective-permute-done.22.refs_3_ = bf16[128,2176]{1,0:T(8,128)(2,1)S(1)} collective-permute-done((bf16[128,2176]{1,0:T(8,128)(2,1)S(1)}, bf16[128,2176]{1,0:T(8,128)(2,1)S(1)}, u32[]{:S(2)}, u32[]{:S(2)}) %collective-permute-start.22) | collective-permute-done | bytes 557088 | tf_op jit(solution)/shard_map/ppermute | solution.py:323
  137.8 5.3 %attend.28 = bf16[128,2176]{1,0:T(8,128)(2,1)S(1)} custom-call(s32[36]{0:T(128)S(1)} %reshape.57.plan_ref, bf16[128,2048]{1,0:T(8,128)(2,1)S(1)} %collective-permute-done.16.refs_0_, bf16[24,256,1024]{2,1,0:T(8,128)(2,1)} %refs_1_.31, bf16[8,256,1024]{2,1,0:T(8,128)(2,1)} %collective-permute-done.15.refs_2_, ...), custom_call_target="tpu_custom_call" | custom-call | flops 1073741824 | bytes 3211264 | tf_op jit(solution)/shard_map/attend/pallas_call | solution.py:161
  146.6 2.6 %collective-permute-done.10.refs_0_ = bf16[128,2048]{1,0:T(8,128)(2,1)} collective-permute-done((bf16[128,2048]{1,0:T(8,128)(2,1)}, bf16[128,2048]{1,0:T(8,128)(2,1)}, u32[]{:S(2)}, u32[]{:S(2)}) %collective-permute-start.10) | collective-permute-done | bytes 524320 | tf_op jit(solution)/shard_map/ppermute | solution.py:309
  149.2 5.1 %attend.20 = bf16[128,2176]{1,0:T(8,128)(2,1)S(1)} custom-call(s32[36]{0:T(128)S(1)} %reshape.56.plan_ref, bf16[128,2048]{1,0:T(8,128)(2,1)} %collective-permute-done.10.refs_0_, bf16[24,256,1024]{2,1,0:T(8,128)(2,1)} %refs_1_.31, bf16[8,256,1024]{2,1,0:T(8,128)(2,1)} %collective-permute-done.refs_2_), custom_call_target="tpu_custom_call" | custom-call | flops 1073741824 | bytes 3211264 | tf_op jit(solution)/shard_map/attend/pallas_call | solution.py:161
  156.3 6.1 %attend.24.refs_0_ = bf16[128,2176]{1,0:T(8,128)(2,1)S(1)} custom-call(s32[36]{0:T(128)S(1)} %reshape.57.plan_ref, bf16[128,2048]{1,0:T(8,128)(2,1)S(1)} %get-tuple-element.16.refs_0_, bf16[24,256,1024]{2,1,0:T(8,128)(2,1)} %refs_1_.31, bf16[8,256,1024]{2,1,0:T(8,128)(2,1)} %collective-permute-done.15.refs_2_, bf16[128,1024]{1,0:T(8,128)(2,1)S(1)} %get-tuple-element.18.refs_3_), custom_call_target="tpu_custom_call" | custom-call | flops 1342177280 | bytes 3735552 | tf_op jit(solution)/shard_map/attend/pallas_call | solution.py:161
  162.4 19.5 %project.2 = bf16[128,8192]{1,0:T(8,128)(2,1)S(1)} custom-call(bf16[128,2176]{1,0:T(8,128)(2,1)S(1)} %attend.24.refs_0_, bf16[128,2176]{1,0:T(8,128)(2,1)S(1)} %collective-permute-done.23.refs_1_, bf16[128,2176]{1,0:T(8,128)(2,1)S(1)} %collective-permute-done.29.refs_2_, bf16[2048,8192]{1,0:T(8,128)(2,1)} %refs_3_.3), custom_call_target="tpu_custom_call" | custom-call | flops 4294967296 | bytes 37748736 | tf_op jit(solution)/shard_map/project/pallas_call | solution.py:227
  183.6 5.0 %attend.17 = bf16[128,2176]{1,0:T(8,128)(2,1)S(1)} custom-call(s32[36]{0:T(128)S(1)} %reshape.56.plan_ref, bf16[128,2048]{1,0:T(8,128)(2,1)S(1)} %collective-permute-done.3.refs_0_, bf16[24,256,1024]{2,1,0:T(8,128)(2,1)} %refs_1_.31, bf16[8,256,1024]{2,1,0:T(8,128)(2,1)} %collective-permute-done.refs_2_), custom_call_target="tpu_custom_call" | custom-call | flops 1073741824 | bytes 3211264 | tf_op jit(solution)/shard_map/attend/pallas_call | solution.py:161
  189.0 5.4 %attend.21 = bf16[128,2176]{1,0:T(8,128)(2,1)S(1)} custom-call(s32[36]{0:T(128)S(1)} %reshape.56.plan_ref, bf16[128,2048]{1,0:T(8,128)(2,1)} %collective-permute-done.9.refs_0_, bf16[24,256,1024]{2,1,0:T(8,128)(2,1)} %refs_1_.31, bf16[8,256,1024]{2,1,0:T(8,128)(2,1)} %collective-permute-done.refs_2_, bf16[128,2176]{1,0:T(8,128)(2,1)S(1)} %collective-permute-done.11.refs_3_), custom_call_target="tpu_custom_call" | custom-call | flops 1073741824 | bytes 3211264 | tf_op jit(solution)/shard_map/attend/pallas_call | solution.py:161
  198.2 5.4 %attend.18 = bf16[128,2176]{1,0:T(8,128)(2,1)S(1)} custom-call(s32[36]{0:T(128)S(1)} %reshape.56.plan_ref, bf16[128,2048]{1,0:T(8,128)(2,1)} %collective-permute-done.2.refs_0_, bf16[24,256,1024]{2,1,0:T(8,128)(2,1)} %refs_1_.31, bf16[8,256,1024]{2,1,0:T(8,128)(2,1)} %collective-permute-done.refs_2_, bf16[128,2176]{1,0:T(8,128)(2,1)S(1)} %collective-permute-done.4.refs_3_), custom_call_target="tpu_custom_call" | custom-call | flops 1073741824 | bytes 3211264 | tf_op jit(solution)/shard_map/attend/pallas_call | solution.py:161
  204.3 5.3 %attend.22 = bf16[128,2176]{1,0:T(8,128)(2,1)S(1)} custom-call(s32[36]{0:T(128)S(1)} %reshape.56.plan_ref, bf16[128,2048]{1,0:T(8,128)(2,1)S(1)} %copy-done.4, bf16[24,256,1024]{2,1,0:T(8,128)(2,1)} %refs_1_.31, bf16[8,256,1024]{2,1,0:T(8,128)(2,1)} %collective-permute-done.refs_2_, bf16[128,2176]{1,0:T(8,128)(2,1)S(1)} %collective-permute-done.12.refs_3_), custom_call_target="tpu_custom_call" | custom-call | flops 1073741824 | bytes 3211264 | tf_op jit(solution)/shard_map/attend/pallas_call | solution.py:161
  214.1 5.4 %attend.19 = bf16[128,2176]{1,0:T(8,128)(2,1)S(1)} custom-call(s32[36]{0:T(128)S(1)} %reshape.56.plan_ref, bf16[128,2048]{1,0:T(8,128)(2,1)} %collective-permute-done.1.refs_0_, bf16[24,256,1024]{2,1,0:T(8,128)(2,1)} %refs_1_.31, bf16[8,256,1024]{2,1,0:T(8,128)(2,1)} %collective-permute-done.refs_2_, bf16[128,2176]{1,0:T(8,128)(2,1)S(1)} %collective-permute-done.5.refs_3_), custom_call_target="tpu_custom_call" | custom-call | flops 1073741824 | bytes 3211264 | tf_op jit(solution)/shard_map/attend/pallas_call | solution.py:161
  220.3 5.3 %attend.23 = bf16[128,2176]{1,0:T(8,128)(2,1)S(1)} custom-call(s32[36]{0:T(128)S(1)} %reshape.56.plan_ref, bf16[128,2048]{1,0:T(8,128)(2,1)S(1)} %copy-done.2, bf16[24,256,1024]{2,1,0:T(8,128)(2,1)} %refs_1_.31, bf16[8,256,1024]{2,1,0:T(8,128)(2,1)} %collective-permute-done.refs_2_, bf16[128,2176]{1,0:T(8,128)(2,1)S(1)} %collective-permute-done.13.refs_3_), custom_call_target="tpu_custom_call" | custom-call | flops 1073741824 | bytes 3211264 | tf_op jit(solution)/shard_map/attend/pallas_call | solution.py:161
  227.5 6.2 %attend.16.refs_0_ = bf16[128,2176]{1,0:T(8,128)(2,1)S(1)} custom-call(s32[36]{0:T(128)S(1)} %reshape.56.plan_ref, bf16[128,2048]{1,0:T(8,128)(2,1)S(1)} %get-tuple-element.17.refs_0_, bf16[24,256,1024]{2,1,0:T(8,128)(2,1)} %refs_1_.31, bf16[8,256,1024]{2,1,0:T(8,128)(2,1)} %collective-permute-done.refs_2_, bf16[128,1024]{1,0:T(8,128)(2,1)S(1)} %get-tuple-element.19.refs_3_), custom_call_target="tpu_custom_call" | custom-call | flops 1342177280 | bytes 3735552 | tf_op jit(solution)/shard_map/attend/pallas_call | solution.py:161
  235.3 20.7 %project.3 = bf16[128,8192]{1,0:T(8,128)(2,1)} custom-call(bf16[128,2176]{1,0:T(8,128)(2,1)S(1)} %attend.16.refs_0_, bf16[128,2176]{1,0:T(8,128)(2,1)S(1)} %collective-permute-done.6.refs_1_, bf16[128,2176]{1,0:T(8,128)(2,1)S(1)} %collective-permute-done.14.refs_2_, bf16[2048,8192]{1,0:T(8,128)(2,1)} %refs_3_.3, ...), custom_call_target="tpu_custom_call" | custom-call | flops 4294967296 | bytes 37748736 | tf_op jit(solution)/shard_map/project/pallas_call | solution.py:227
  (94 shorter events, 50.4 us)
Async XLA Ops:
  9.4 55.8 %collective-permute-start.15 = (bf16[8,256,1024]{2,1,0:T(8,128)(2,1)}, bf16[8,256,1024]{2,1,0:T(8,128)(2,1)}, u32[]{:S(2)}, u32[]{:S(2)}) collective-permute-start(bf16[8,256,1024]{2,1,0:T(8,128)(2,1)} %pack_blocks.3), channel_id=1, source_target_pairs={{0,2},{2,0},{4,6},{6,4},{8,10},{10,8},{12,14},{14,12},{16,18},{18,... | collective-permute-start | bytes 12582920 | tf_op jit(solution)/shard_map/ppermute | solution.py:300
  10.4 15.1 %collective-permute-start.16 = (bf16[128,2048]{1,0:T(8,128)(2,1)S(1)}, bf16[128,2048]{1,0:T(8,128)(2,1)S(1)}, u32[]{:S(2)}, u32[]{:S(2)}) collective-permute-start(bf16[128,2048]{1,0:T(8,128)(2,1)S(1)} %get-tuple-element.16.refs_0_), channel_id=1, source_target_pairs={{0,8},{2,10},{8,16},{10,18},{16,24},{18,26},{24,28},{26,30},{28,20... | collective-permute-start | bytes 1572872 | tf_op jit(solution)/shard_map/ppermute | solution.py:309
  13.2 40.0 %copy-start.5 = (s32[8]{0:T(128)S(1)}, s32[8]{0:T(128)}, u32[]{:S(2)}) copy-start(s32[8]{0:T(128)} %constant.198.clone) | copy-start | bytes 100
  20.6 128.5 %collective-permute-start = (bf16[8,256,1024]{2,1,0:T(8,128)(2,1)}, bf16[8,256,1024]{2,1,0:T(8,128)(2,1)}, u32[]{:S(2)}, u32[]{:S(2)}) collective-permute-start(bf16[8,256,1024]{2,1,0:T(8,128)(2,1)} %pack_blocks.2), channel_id=1, source_target_pairs={{0,2},{2,0},{4,6},{6,4},{8,10},{10,8},{12,14},{14,12},{16,18},{18,... | collective-permute-start | bytes 12582920 | tf_op jit(solution)/shard_map/ppermute | solution.py:300
  25.5 13.8 %collective-permute-start.17 = (bf16[128,2048]{1,0:T(8,128)(2,1)S(1)}, bf16[128,2048]{1,0:T(8,128)(2,1)S(1)}, u32[]{:S(2)}, u32[]{:S(2)}) collective-permute-start(bf16[128,2048]{1,0:T(8,128)(2,1)S(1)} %collective-permute-done.16.refs_0_), channel_id=1, source_target_pairs={{0,8},{2,10},{8,16},{10,18},{16,24},{18,26},{24,28},{26,30},{28,20... | collective-permute-start | bytes 1572872 | tf_op jit(solution)/shard_map/ppermute | solution.py:309
  27.4 15.3 %collective-permute-start.24 = (bf16[128,2048]{1,0:T(8,128)(2,1)S(1)}, bf16[128,2048]{1,0:T(8,128)(2,1)S(1)}, u32[]{:S(2)}, u32[]{:S(2)}) collective-permute-start(bf16[128,2048]{1,0:T(8,128)(2,1)S(1)} %get-tuple-element.16.refs_0_), channel_id=1, source_target_pairs={{8,0},{10,2},{16,8},{18,10},{24,16},{26,18},{28,24},{30,26},{20,28... | collective-permute-start | bytes 1572872 | tf_op jit(solution)/shard_map/ppermute | solution.py:309
  39.3 13.0 %collective-permute-start.18 = (bf16[128,2048]{1,0:T(8,128)(2,1)S(1)}, bf16[128,2048]{1,0:T(8,128)(2,1)}, u32[]{:S(2)}, u32[]{:S(2)}) collective-permute-start(bf16[128,2048]{1,0:T(8,128)(2,1)S(1)} %collective-permute-done.17.refs_0_), channel_id=1, source_target_pairs={{0,8},{2,10},{8,16},{10,18},{16,24},{18,26},{24,28},{26,30},{28,20... | collective-permute-start | bytes 1572872 | tf_op jit(solution)/shard_map/ppermute | solution.py:309
  40.7 31.1 %collective-permute-start.7 = (bf16[128,2048]{1,0:T(8,128)(2,1)S(1)}, bf16[128,2048]{1,0:T(8,128)(2,1)S(1)}, u32[]{:S(2)}, u32[]{:S(2)}) collective-permute-start(bf16[128,2048]{1,0:T(8,128)(2,1)S(1)} %get-tuple-element.17.refs_0_), channel_id=1, source_target_pairs={{8,0},{10,2},{16,8},{18,10},{24,16},{26,18},{28,24},{30,26},{20,28... | collective-permute-start | bytes 1572872 | tf_op jit(solution)/shard_map/ppermute | solution.py:309
  42.7 21.8 %collective-permute-start.25 = (bf16[128,2048]{1,0:T(8,128)(2,1)S(1)}, bf16[128,2048]{1,0:T(8,128)(2,1)}, u32[]{:S(2)}, u32[]{:S(2)}) collective-permute-start(bf16[128,2048]{1,0:T(8,128)(2,1)S(1)} %collective-permute-done.24.refs_0_), channel_id=1, source_target_pairs={{8,0},{10,2},{16,8},{18,10},{24,16},{26,18},{28,24},{30,26},{20,28... | collective-permute-start | bytes 1572872 | tf_op jit(solution)/shard_map/ppermute | solution.py:309
  52.3 13.0 %collective-permute-start.19 = (bf16[128,2048]{1,0:T(8,128)(2,1)}, bf16[128,2048]{1,0:T(8,128)(2,1)}, u32[]{:S(2)}, u32[]{:S(2)}) collective-permute-start(bf16[128,2048]{1,0:T(8,128)(2,1)} %collective-permute-done.18.refs_0_), channel_id=1, source_target_pairs={{0,8},{2,10},{8,16},{10,18},{16,24},{18,26},{24,28},{26,30},{28,20... | collective-permute-start | bytes 1572872 | tf_op jit(solution)/shard_map/ppermute | solution.py:309
  64.5 15.1 %collective-permute-start.26 = (bf16[128,2048]{1,0:T(8,128)(2,1)}, bf16[128,2048]{1,0:T(8,128)(2,1)S(1)}, u32[]{:S(2)}, u32[]{:S(2)}) collective-permute-start(bf16[128,2048]{1,0:T(8,128)(2,1)} %collective-permute-done.25.refs_0_), channel_id=1, source_target_pairs={{8,0},{10,2},{16,8},{18,10},{24,16},{26,18},{28,24},{30,26},{20,28... | collective-permute-start | bytes 1572872 | tf_op jit(solution)/shard_map/ppermute | solution.py:309
  70.4 21.1 %collective-permute-start.20 = (bf16[128,2176]{1,0:T(8,128)(2,1)S(1)}, bf16[128,2176]{1,0:T(8,128)(2,1)S(1)}, u32[]{:S(2)}, u32[]{:S(2)}) collective-permute-start(bf16[128,2176]{1,0:T(8,128)(2,1)S(1)} %attend.25), channel_id=1, source_target_pairs={{8,0},{10,2},{16,8},{18,10},{24,16},{26,18},{28,24},{30,26},{20,28... | collective-permute-start | bytes 1671176 | tf_op jit(solution)/shard_map/ppermute | solution.py:323
  71.8 31.0 %collective-permute-start.8 = (bf16[128,2048]{1,0:T(8,128)(2,1)S(1)}, bf16[128,2048]{1,0:T(8,128)(2,1)S(1)}, u32[]{:S(2)}, u32[]{:S(2)}) collective-permute-start(bf16[128,2048]{1,0:T(8,128)(2,1)S(1)} %collective-permute-done.7.refs_0_), channel_id=1, source_target_pairs={{8,0},{10,2},{16,8},{18,10},{24,16},{26,18},{28,24},{30,26},{20,28... | collective-permute-start | bytes 1572872 | tf_op jit(solution)/shard_map/ppermute | solution.py:309
  84.6 18.9 %collective-permute-start.27 = (bf16[128,2176]{1,0:T(8,128)(2,1)S(1)}, bf16[128,2176]{1,0:T(8,128)(2,1)S(1)}, u32[]{:S(2)}, u32[]{:S(2)}) collective-permute-start(bf16[128,2176]{1,0:T(8,128)(2,1)S(1)} %attend.29), channel_id=1, source_target_pairs={{0,8},{2,10},{8,16},{10,18},{16,24},{18,26},{24,28},{26,30},{28,20... | collective-permute-start | bytes 1671176 | tf_op jit(solution)/shard_map/ppermute | solution.py:323
  96.9 17.7 %collective-permute-start.21 = (bf16[128,2176]{1,0:T(8,128)(2,1)S(1)}, bf16[128,2176]{1,0:T(8,128)(2,1)S(1)}, u32[]{:S(2)}, u32[]{:S(2)}) collective-permute-start(bf16[128,2176]{1,0:T(8,128)(2,1)S(1)} %attend.26), channel_id=1, source_target_pairs={{8,0},{10,2},{16,8},{18,10},{24,16},{26,18},{28,24},{30,26},{20,28... | collective-permute-start | bytes 1671176 | tf_op jit(solution)/shard_map/ppermute | solution.py:323
  97.8 23.1 %collective-permute-start.1 = (bf16[128,2048]{1,0:T(8,128)(2,1)S(1)}, bf16[128,2048]{1,0:T(8,128)(2,1)}, u32[]{:S(2)}, u32[]{:S(2)}) collective-permute-start(bf16[128,2048]{1,0:T(8,128)(2,1)S(1)} %get-tuple-element.17.refs_0_), channel_id=1, source_target_pairs={{0,8},{2,10},{8,16},{10,18},{16,24},{18,26},{24,28},{26,30},{28,20... | collective-permute-start | bytes 1572872 | tf_op jit(solution)/shard_map/ppermute | solution.py:309
  102.7 23.3 %collective-permute-start.9 = (bf16[128,2048]{1,0:T(8,128)(2,1)S(1)}, bf16[128,2048]{1,0:T(8,128)(2,1)}, u32[]{:S(2)}, u32[]{:S(2)}) collective-permute-start(bf16[128,2048]{1,0:T(8,128)(2,1)S(1)} %collective-permute-done.8.refs_0_), channel_id=1, source_target_pairs={{8,0},{10,2},{16,8},{18,10},{24,16},{26,18},{28,24},{30,26},{20,28... | collective-permute-start | bytes 1572872 | tf_op jit(solution)/shard_map/ppermute | solution.py:309
  109.0 17.8 %collective-permute-start.28 = (bf16[128,2176]{1,0:T(8,128)(2,1)S(1)}, bf16[128,2176]{1,0:T(8,128)(2,1)S(1)}, u32[]{:S(2)}, u32[]{:S(2)}) collective-permute-start(bf16[128,2176]{1,0:T(8,128)(2,1)S(1)} %attend.30), channel_id=1, source_target_pairs={{0,8},{2,10},{8,16},{10,18},{16,24},{18,26},{24,28},{26,30},{28,20... | collective-permute-start | bytes 1671176 | tf_op jit(solution)/shard_map/ppermute | solution.py:323
  120.0 17.8 %collective-permute-start.22 = (bf16[128,2176]{1,0:T(8,128)(2,1)S(1)}, bf16[128,2176]{1,0:T(8,128)(2,1)S(1)}, u32[]{:S(2)}, u32[]{:S(2)}) collective-permute-start(bf16[128,2176]{1,0:T(8,128)(2,1)S(1)} %attend.27), channel_id=1, source_target_pairs={{8,0},{10,2},{16,8},{18,10},{24,16},{26,18},{28,24},{30,26},{20,28... | collective-permute-start | bytes 1671176 | tf_op jit(solution)/shard_map/ppermute | solution.py:323
  120.9 24.4 %collective-permute-start.2 = (bf16[128,2048]{1,0:T(8,128)(2,1)}, bf16[128,2048]{1,0:T(8,128)(2,1)}, u32[]{:S(2)}, u32[]{:S(2)}) collective-permute-start(bf16[128,2048]{1,0:T(8,128)(2,1)} %collective-permute-done.1.refs_0_), channel_id=1, source_target_pairs={{0,8},{2,10},{8,16},{10,18},{16,24},{18,26},{24,28},{26,30},{28,20... | collective-permute-start | bytes 1572872 | tf_op jit(solution)/shard_map/ppermute | solution.py:309
  126.0 23.2 %collective-permute-start.10 = (bf16[128,2048]{1,0:T(8,128)(2,1)}, bf16[128,2048]{1,0:T(8,128)(2,1)}, u32[]{:S(2)}, u32[]{:S(2)}) collective-permute-start(bf16[128,2048]{1,0:T(8,128)(2,1)} %collective-permute-done.9.refs_0_), channel_id=1, source_target_pairs={{8,0},{10,2},{16,8},{18,10},{24,16},{26,18},{28,24},{30,26},{20,28... | collective-permute-start | bytes 1572872 | tf_op jit(solution)/shard_map/ppermute | solution.py:309
  132.2 30.2 %collective-permute-start.29 = (bf16[128,2176]{1,0:T(8,128)(2,1)S(1)}, bf16[128,2176]{1,0:T(8,128)(2,1)S(1)}, u32[]{:S(2)}, u32[]{:S(2)}) collective-permute-start(bf16[128,2176]{1,0:T(8,128)(2,1)S(1)} %attend.31), channel_id=1, source_target_pairs={{0,8},{2,10},{8,16},{10,18},{16,24},{18,26},{24,28},{26,30},{28,20... | collective-permute-start | bytes 1671176 | tf_op jit(solution)/shard_map/ppermute | solution.py:323
  143.2 19.2 %collective-permute-start.23 = (bf16[128,2176]{1,0:T(8,128)(2,1)S(1)}, bf16[128,2176]{1,0:T(8,128)(2,1)S(1)}, u32[]{:S(2)}, u32[]{:S(2)}) collective-permute-start(bf16[128,2176]{1,0:T(8,128)(2,1)S(1)} %attend.28), channel_id=1, source_target_pairs={{8,0},{10,2},{16,8},{18,10},{24,16},{26,18},{28,24},{30,26},{20,28... | collective-permute-start | bytes 1671176 | tf_op jit(solution)/shard_map/ppermute | solution.py:323
  145.3 38.3 %collective-permute-start.3 = (bf16[128,2048]{1,0:T(8,128)(2,1)}, bf16[128,2048]{1,0:T(8,128)(2,1)S(1)}, u32[]{:S(2)}, u32[]{:S(2)}) collective-permute-start(bf16[128,2048]{1,0:T(8,128)(2,1)} %collective-permute-done.2.refs_0_), channel_id=1, source_target_pairs={{0,8},{2,10},{8,16},{10,18},{16,24},{18,26},{24,28},{26,30},{28,20... | collective-permute-start | bytes 1572872 | tf_op jit(solution)/shard_map/ppermute | solution.py:309
  154.3 34.7 %collective-permute-start.11 = (bf16[128,2176]{1,0:T(8,128)(2,1)S(1)}, bf16[128,2176]{1,0:T(8,128)(2,1)S(1)}, u32[]{:S(2)}, u32[]{:S(2)}) collective-permute-start(bf16[128,2176]{1,0:T(8,128)(2,1)S(1)} %attend.20), channel_id=1, source_target_pairs={{0,8},{2,10},{8,16},{10,18},{16,24},{18,26},{24,28},{26,30},{28,20... | collective-permute-start | bytes 1671176 | tf_op jit(solution)/shard_map/ppermute | solution.py:323
  181.9 53.4 %collective-permute-start.30 = (bf16[128,8192]{1,0:T(8,128)(2,1)S(1)}, bf16[128,8192]{1,0:T(8,128)(2,1)S(1)}, u32[]{:S(2)}, u32[]{:S(2)}) collective-permute-start(bf16[128,8192]{1,0:T(8,128)(2,1)S(1)} %project.2), channel_id=1, source_target_pairs={{0,1},{1,0},{2,3},{3,2},{4,5},{5,4},{6,7},{7,6},{8,9},{9,8},{10,11... | collective-permute-start | bytes 6291464 | tf_op jit(solution)/shard_map/ppermute | solution.py:330
  188.7 9.6 %collective-permute-start.4 = (bf16[128,2176]{1,0:T(8,128)(2,1)S(1)}, bf16[128,2176]{1,0:T(8,128)(2,1)S(1)}, u32[]{:S(2)}, u32[]{:S(2)}) collective-permute-start(bf16[128,2176]{1,0:T(8,128)(2,1)S(1)} %attend.17), channel_id=1, source_target_pairs={{8,0},{10,2},{16,8},{18,10},{24,16},{26,18},{28,24},{30,26},{20,28... | collective-permute-start | bytes 1671176 | tf_op jit(solution)/shard_map/ppermute | solution.py:323
  194.4 9.9 %collective-permute-start.12 = (bf16[128,2176]{1,0:T(8,128)(2,1)S(1)}, bf16[128,2176]{1,0:T(8,128)(2,1)S(1)}, u32[]{:S(2)}, u32[]{:S(2)}) collective-permute-start(bf16[128,2176]{1,0:T(8,128)(2,1)S(1)} %attend.21), channel_id=1, source_target_pairs={{0,8},{2,10},{8,16},{10,18},{16,24},{18,26},{24,28},{26,30},{28,20... | collective-permute-start | bytes 1671176 | tf_op jit(solution)/shard_map/ppermute | solution.py:323
  203.7 10.4 %collective-permute-start.5 = (bf16[128,2176]{1,0:T(8,128)(2,1)S(1)}, bf16[128,2176]{1,0:T(8,128)(2,1)S(1)}, u32[]{:S(2)}, u32[]{:S(2)}) collective-permute-start(bf16[128,2176]{1,0:T(8,128)(2,1)S(1)} %attend.18), channel_id=1, source_target_pairs={{8,0},{10,2},{16,8},{18,10},{24,16},{26,18},{28,24},{30,26},{20,28... | collective-permute-start | bytes 1671176 | tf_op jit(solution)/shard_map/ppermute | solution.py:323
  209.7 10.7 %collective-permute-start.13 = (bf16[128,2176]{1,0:T(8,128)(2,1)S(1)}, bf16[128,2176]{1,0:T(8,128)(2,1)S(1)}, u32[]{:S(2)}, u32[]{:S(2)}) collective-permute-start(bf16[128,2176]{1,0:T(8,128)(2,1)S(1)} %attend.22), channel_id=1, source_target_pairs={{0,8},{2,10},{8,16},{10,18},{16,24},{18,26},{24,28},{26,30},{28,20... | collective-permute-start | bytes 1671176 | tf_op jit(solution)/shard_map/ppermute | solution.py:323
  219.5 14.2 %collective-permute-start.6 = (bf16[128,2176]{1,0:T(8,128)(2,1)S(1)}, bf16[128,2176]{1,0:T(8,128)(2,1)S(1)}, u32[]{:S(2)}, u32[]{:S(2)}) collective-permute-start(bf16[128,2176]{1,0:T(8,128)(2,1)S(1)} %attend.19), channel_id=1, source_target_pairs={{8,0},{10,2},{16,8},{18,10},{24,16},{26,18},{28,24},{30,26},{20,28... | collective-permute-start | bytes 1671176 | tf_op jit(solution)/shard_map/ppermute | solution.py:323
  225.7 9.6 %collective-permute-start.14 = (bf16[128,2176]{1,0:T(8,128)(2,1)S(1)}, bf16[128,2176]{1,0:T(8,128)(2,1)S(1)}, u32[]{:S(2)}, u32[]{:S(2)}) collective-permute-start(bf16[128,2176]{1,0:T(8,128)(2,1)S(1)} %attend.23), channel_id=1, source_target_pairs={{0,8},{2,10},{8,16},{10,18},{16,24},{18,26},{24,28},{26,30},{28,20... | collective-permute-start | bytes 1671176 | tf_op jit(solution)/shard_map/ppermute | solution.py:323
  (8 other events, 112.9 us)

commit v2 on v1

v2 whole, which is shorter than its diff:
```python
import functools

import jax
import jax.numpy as jnp
from jax import lax
from jax.experimental import pallas as pl
from jax.experimental.pallas import tpu as pltpu
from jax.sharding import PartitionSpec as P

HEAD_SIZE = 128
NEW_TOKEN_COUNT = 128
PREFIX_BLOCK_LEN = 256
MAXB = 16
LOG2E = 1.4426950408889634
SCALE2 = HEAD_SIZE ** (-0.5) * LOG2E
NEG = -1e30
F32 = jnp.float32
BF16 = jnp.bfloat16
TOK = NEW_TOKEN_COUNT
STAT = 128


def dot_nt(a, b):
    return lax.dot_general(a, b, (((1,), (1,)), ((), ())), preferred_element_type=F32)


def chip_ring(nchips):
    if nchips % 2:
        return list(range(nchips))
    up = list(range(0, nchips, 2))
    return up + [chip + 1 for chip in reversed(up)]


def attend_kernel(call, group, heads, unroll, has_carry, has_fresh, plan_ref, *refs):
    refs = list(refs)
    q_ref, own_ref, sib_ref = refs[:3]
    rest = refs[3:]
    fresh_ref = rest.pop(0) if has_fresh else None
    carry_ref, carry_stat_ref = (rest.pop(0), rest.pop(0)) if has_carry else (None, None)
    out_ref, stat_ref = rest
    step = pl.program_id(0)
    width = group * HEAD_SIZE
    pair = 2 * HEAD_SIZE
    stat_at = heads * HEAD_SIZE
    n_own = plan_ref[4 * call + 2]
    n_sib = plan_ref[4 * call + 3]

    col = lax.broadcasted_iota(jnp.int32, (1, PREFIX_BLOCK_LEN), 1)
    biases = [
        jnp.where(col < n_own, 0.0, NEG).astype(F32),
        jnp.where(col < n_sib, 0.0, NEG).astype(F32),
    ]
    if has_fresh:
        tok = lax.broadcasted_iota(jnp.int32, (TOK, TOK), 0)
        new = lax.broadcasted_iota(jnp.int32, (TOK, TOK), 1)
        causal = jnp.where(new <= tok, 0.0, NEG).astype(F32)
        biases.append(jnp.concatenate([causal] * group, axis=0))
    lane = lax.rem(lax.broadcasted_iota(jnp.int32, (TOK, STAT), 1), heads)
    if has_carry:
        full_lane = lax.broadcasted_iota(jnp.int32, (TOK, STAT), 1)
        stat_in = jnp.where(full_lane < 3 * heads, carry_stat_ref[...].astype(F32), 0.0)
    stat = stat_ref[...]

    for u in range(unroll):
        q = jnp.concatenate(
            [
                q_ref[:, u * width + g * HEAD_SIZE : u * width + (g + 1) * HEAD_SIZE]
                for g in range(group)
            ],
            axis=0,
        )
        blocks = [own_ref[0, :, u * pair : (u + 1) * pair], sib_ref[0, :, u * pair : (u + 1) * pair]]
        if has_fresh:
            blocks.append(fresh_ref[:, u * pair : (u + 1) * pair])
        scores = [dot_nt(q, x[:, :HEAD_SIZE]) + bias for x, bias in zip(blocks, biases)]
        top = functools.reduce(
            jnp.maximum, [jnp.max(x, axis=1, keepdims=True) for x in scores]
        )
        probs = jnp.concatenate(
            [jnp.exp2((x - top) * SCALE2).astype(BF16) for x in scores], axis=1
        )
        values = jnp.concatenate([x[:, HEAD_SIZE:] for x in blocks], axis=0)
        values = jnp.concatenate([values, jnp.ones_like(values)], axis=1)
        mixed = jnp.dot(probs, values, preferred_element_type=F32)
        base = top * SCALE2
        for g in range(group):
            rows = slice(g * TOK, (g + 1) * TOK)
            head = (step * unroll + u) * group + g
            o_g, total, base_g = mixed[rows, :HEAD_SIZE], mixed[rows, HEAD_SIZE:], base[rows]
            if has_carry:
                lse_c = jnp.sum(jnp.where(lane == head, stat_in, 0.0), axis=1, keepdims=True)
                at = u * width + g * HEAD_SIZE
                o_c = carry_ref[:, at : at + HEAD_SIZE].astype(F32)
                high = jnp.maximum(base_g, lse_c)
                w_c = jnp.exp2(lse_c - high)
                w_g = jnp.exp2(base_g - high)
                total = w_c + total * w_g
                o_g = o_c * w_c + o_g * w_g
                base_g = high
            stat = jnp.where(lane == head, base_g + jnp.log2(total), stat)
            at = pl.multiple_of(step * unroll * width, width) + (u * width + g * HEAD_SIZE)
            at = pl.multiple_of(at, HEAD_SIZE)
            out_ref[:, pl.ds(at, HEAD_SIZE)] = (o_g / total).astype(BF16)
    stat_ref[...] = stat

    @pl.when(step == pl.num_programs(0) - 1)
    def _():
        full = lax.broadcasted_iota(jnp.int32, (TOK, STAT), 1)
        first = stat.astype(BF16).astype(F32)
        second = (stat - first).astype(BF16).astype(F32)
        third = stat - first - second
        split = jnp.where(full < heads, first, jnp.where(full < 2 * heads, second, third))
        out_ref[:, stat_at : stat_at + STAT] = split.astype(BF16)


def attend(call, plan, q, store, sib, kv_local, fresh=None, carry=None):
    heads = q.shape[1] // HEAD_SIZE
    group = heads // kv_local
    unroll = 2 if kv_local % 2 == 0 else 1
    width = unroll * group * HEAD_SIZE
    pair = unroll * 2 * HEAD_SIZE
    cols = heads * HEAD_SIZE + STAT
    span = 2 * PREFIX_BLOCK_LEN + (TOK if fresh is not None else 0)
    in_specs = [
        pl.BlockSpec((TOK, width), lambda h, plan: (0, h)),
        pl.BlockSpec((1, PREFIX_BLOCK_LEN, pair), lambda h, plan: (plan[4 * call], 0, h)),
        pl.BlockSpec((1, PREFIX_BLOCK_LEN, pair), lambda h, plan: (plan[4 * call + 1], 0, h)),
    ]
    args = [q, store, sib]
    if fresh is not None:
        in_specs.append(pl.BlockSpec((TOK, pair), lambda h, plan: (0, h)))
        args.append(fresh)
    if carry is not None:
        in_specs.append(pl.BlockSpec((TOK, width), lambda h, plan: (0, h)))
        in_specs.append(pl.BlockSpec((TOK, STAT), lambda h, plan: (0, heads)))
        args += [carry, carry]
    body = functools.partial(
        attend_kernel, call, group, heads, unroll, carry is not None, fresh is not None
    )
    return pl.pallas_call(
        body,
        out_shape=jax.ShapeDtypeStruct((TOK, cols), BF16),
        grid_spec=pltpu.PrefetchScalarGridSpec(
            num_scalar_prefetch=1,
            grid=(kv_local // unroll,),
            in_specs=in_specs,
            out_specs=pl.BlockSpec((TOK, cols), lambda h, plan: (0, 0)),
            scratch_shapes=[pltpu.VMEM((TOK, STAT), F32)],
        ),
        compiler_params=pltpu.CompilerParams(vmem_limit_bytes=40 * 1024 * 1024),
        cost_estimate=pl.CostEstimate(
            flops=8 * heads * TOK * span * HEAD_SIZE,
            bytes_accessed=4 * TOK * cols + 4 * kv_local * span * 2 * HEAD_SIZE,
            transcendentals=heads * TOK * span,
        ),
        name="attend",
    )(plan, *args)


def merge_parts(heads, part_refs, attn_ref):
    stat_at = heads * HEAD_SIZE
    lses = []
    for ref in part_refs:
        s = ref[:, stat_at : stat_at + STAT].astype(F32)
        lses.append(s[:, :heads] + s[:, heads : 2 * heads] + s[:, 2 * heads : 3 * heads])
    high = functools.reduce(jnp.maximum, lses)
    weights = [jnp.exp2(x - high) for x in lses]
    norm = 1.0 / functools.reduce(jnp.add, weights)
    weights = [w * norm for w in weights]
    for head in range(heads):
        cols = slice(head * HEAD_SIZE, (head + 1) * HEAD_SIZE)
        mixed = functools.reduce(
            jnp.add,
            [w[:, head : head + 1] * ref[:, cols].astype(F32) for w, ref in zip(weights, part_refs)],
        )
        attn_ref[:, cols] = mixed.astype(BF16)


def project_kernel(heads, nparts, nweight, nadd, *refs):
    part_refs = refs[:nparts]
    w_refs = refs[nparts : nparts + nweight]
    add_refs = refs[nparts + nweight : nparts + nweight + nadd]
    out_ref, attn_ref = refs[nparts + nweight + nadd :]

    @pl.when(pl.program_id(0) == 0)
    def _():
        merge_parts(heads, part_refs, attn_ref)

    depth = w_refs[0].shape[0]
    got = functools.reduce(
        jnp.add,
        [
            jnp.dot(
                attn_ref[:, i * depth : (i + 1) * depth], ref[...], preferred_element_type=F32
            )
            for i, ref in enumerate(w_refs)
        ],
    ).astype(BF16)
    if nadd:
        total = got.astype(F32)
        for ref in add_refs:
            total = total + ref[...].astype(F32)
        got = total.astype(BF16)
    out_ref[...] = got


def project(parts, weight, adds=()):
    depth, model = weight.shape
    heads = depth // HEAD_SIZE
    cols = parts[0].shape[1]
    tile = 1024
    streams = 4 if depth % (4 * HEAD_SIZE) == 0 else 1
    in_specs = [pl.BlockSpec((TOK, cols), lambda j: (0, 0)) for _ in parts]
    for i in range(streams):
        in_specs.append(pl.BlockSpec((depth // streams, tile), lambda j, i=i: (i, j)))
    in_specs += [pl.BlockSpec((TOK, tile), lambda j: (0, j)) for _ in adds]
    return pl.pallas_call(
        functools.partial(project_kernel, heads, len(parts), streams, len(adds)),
        out_shape=jax.ShapeDtypeStruct((TOK, model), BF16),
        grid=(model // tile,),
        in_specs=in_specs,
        out_specs=pl.BlockSpec((TOK, tile), lambda j: (0, j)),
        scratch_shapes=[pltpu.VMEM((TOK, depth), BF16)],
        compiler_params=pltpu.CompilerParams(vmem_limit_bytes=40 * 1024 * 1024),
        cost_estimate=pl.CostEstimate(
            flops=2 * TOK * depth * model,
            bytes_accessed=2 * depth * model + 4 * TOK * model,
            transcendentals=0,
        ),
        name="project",
    )(*parts, *([weight] * streams), *adds)


def shards(
    queries, new_key_values, key_value_store, o_weight, residual, hit_dev, hit_blk, prefix_len
):
    npool = lax.axis_size("pool")
    ntp = lax.axis_size("tp")
    me = lax.axis_index("pool")
    tp = lax.axis_index("tp")
    rdev = queries.shape[0] // TOK
    kv_local = key_value_store.shape[2] // (2 * HEAD_SIZE)
    nchips = npool // 2
    core = lax.rem(me, 2)
    chip = lax.div(me, 2)
    sibling = me + 1 - 2 * core
    ring = chip_ring(nchips)
    place = [ring.index(i) for i in range(nchips)]
    split_rows = ntp == rdev and rdev == 2

    swap_perm = [(p, p + 1 - 2 * (p % 2)) for p in range(npool)]
    cw_perm, ccw_perm = [], []
    for k in range(nchips):
        a, b = ring[k], ring[(k + 1) % nchips]
        for c in range(2):
            cw_perm.append((2 * a + c, 2 * b + c))
            ccw_perm.append((2 * b + c, 2 * a + c))

    starts = jnp.arange(MAXB, dtype=jnp.int32)[None, :] * PREFIX_BLOCK_LEN
    left = jnp.clip(prefix_len[:, None] - starts, 0, PREFIX_BLOCK_LEN)
    here, beside = hit_dev == me, hit_dev == sibling
    table = jnp.stack(
        [
            jnp.sum(jnp.where(at, x, 0), axis=1)
            for x, at in ((hit_blk, here), (hit_blk, beside), (left, here), (left, beside))
        ],
        axis=1,
    )
    half = nchips // 2
    steps = list(range(-half, half + 1))
    spot = jnp.asarray(place, jnp.int32)[chip]
    chips_at = jnp.asarray(ring, jnp.int32)[
        lax.rem(spot + nchips - jnp.asarray(steps, jnp.int32), nchips)
    ]
    slots = [1 - tp, tp] if split_rows else [jnp.int32(i) for i in range(rdev)]
    wanted = ((chips_at * 2 + core) * rdev)[None, :] + jnp.stack(slots)[:, None]
    plans = jnp.take(table, wanted.reshape(-1), axis=0, mode="clip").reshape(rdev, -1)
    sib = lax.ppermute(key_value_store, "pool", swap_perm)

    state = []
    for order, slot in enumerate(slots):
        plan = plans[order]
        q = lax.dynamic_slice_in_dim(queries, slot * TOK, TOK, 0)
        fresh = lax.dynamic_slice_in_dim(new_key_values, slot * TOK, TOK, 0)
        if nchips % 2:
            reach = (half, half)
        else:
            reach = (half, half - 1) if order % 2 == 0 else (half - 1, half)
        held = {}
        for sign, perm, hops in ((1, cw_perm, reach[0]), (-1, ccw_perm, reach[1])):
            moving = q
            for s in range(1, hops + 1):
                moving = lax.ppermute(moving, "pool", perm)
                held[sign * s] = moving
        state.append((plan, q, fresh, reach, held))

    parts_of = []
    for plan, q, fresh, reach, held in state:
        run = functools.partial(attend, store=key_value_store, sib=sib, kv_local=kv_local)
        call = lambda s: steps.index(s)
        own = run(call(0), plan, q, fresh=fresh)
        parts = [own]
        for sign, back, hops in ((1, ccw_perm, reach[0]), (-1, cw_perm, reach[1])):
            carry = None
            for s in range(hops, 0, -1):
                carry = run(call(sign * s), plan, held[sign * s], carry=carry)
                carry = lax.ppermute(carry, "pool", back)
            if carry is not None:
                parts.append(carry)
        parts_of.append(parts)

    if split_rows:
        away = project(parts_of[0], o_weight)
        got = lax.ppermute(away, "tp", [(0, 1), (1, 0)])
        return project(parts_of[1], o_weight, (got, residual))
    rows = jnp.concatenate([project(parts, o_weight) for parts in parts_of], axis=0)
    mine = lax.psum_scatter(rows, "tp", scatter_dimension=0, tiled=True)
    return (mine.astype(F32) + residual.astype(F32)).astype(BF16)


def solution(mesh):
    placed = (
        P("pool", "tp"),
        P("pool", "tp"),
        P("pool", None, "tp"),
        P("tp", None),
        P(("pool", "tp"), None),
        P(),
        P(),
        P(),
    )
    return jax.shard_map(
        shards, mesh=mesh, in_specs=placed, out_specs=P(("pool", "tp"), None), check_vma=False
    )
```

time: 258 us -> 246 us (0.953)
  Pallas kernels: 141 us -> 94.5 us
  waiting for transfers between devices: 67.7 us -> 87.8 us
  local copies, waits for them, and re-layouts: 8.89 us -> 27.4 us
    pallas_call x4 -> x2, Pallas kernels: 54.6 us -> 30.4 us  [project(): pl.pallas_call(functools.partial(project_kernel, heads, len(parts), strea...]
    unnamed x18 -> x36, local copies, waits for them, and re-layouts: 0.04 us -> 22.9 us
    pallas_call x16, Pallas kernels: 86.4 us -> 64.1 us  [attend(): pl.pallas_call(body, out_shape=jax.ShapeDtypeStruct((TOK, cols), BF16), g...]
    ppermute x14, waiting for transfers between devices: 20.8 us -> 33.2 us  [shards(): carry = lax.ppermute(carry, 'pool', back)]
    ppermute x14, waiting for transfers between devices: 46.9 us -> 54.6 us  [shards(): moving = lax.ppermute(moving, 'pool', perm)]
    gather x7 -> x2, local copies, waits for them, and re-layouts: 4.65 us -> 1.22 us  [the longest x1 0.66 us: shards(): jnp.asarray(ring, jnp.int32)]
  transfers between devices with their start and end apart: 31 -> 30, of which waited for: 16 -> 14; matrix products, arithmetic and copies ran while one was open for 3% -> 2% of each run, Pallas kernels for 44% -> 32%
where the time goes in v2:
time: 246 us; the launch traced here: 245 us
  Pallas kernels  94.5 us (38%)
  waiting for transfers between devices  87.8 us (36%)
  starting transfers between devices  34.2 us (14%)
  local copies, waits for them, and re-layouts  27.4 us (11%)
    pallas_call x16, Pallas kernels, attend(): pl.pallas_call(body, out_shape=jax.ShapeDtypeStruct((TOK, cols), BF16), g...  64.1 us
    ppermute x14, waiting for transfers between devices, shards(): moving = lax.ppermute(moving, 'pool', perm)  54.6 us
    ppermute x14, waiting for transfers between devices, shards(): carry = lax.ppermute(carry, 'pool', back)  33.2 us
    pallas_call x2, Pallas kernels, project(): pl.pallas_call(functools.partial(project_kernel, heads, len(parts), strea...  30.4 us
    unnamed x36, local copies, waits for them, and re-layouts  22.9 us
    ppermute x14, starting transfers between devices, shards(): moving = lax.ppermute(moving, 'pool', perm)  17.4 us
    ppermute x14, starting transfers between devices, shards(): carry = lax.ppermute(carry, 'pool', back)  14.7 us
  transfers between devices with their start and end apart: 30, of which 14 were waited for; matrix products, arithmetic and copies ran while one was open for 2% of the time, Pallas kernels for 32%

profile of v2, /device:TPU:0, one launch (start us, length us, event | category | flops | bytes accessed | tf_op | source)
XLA Modules:
  0.0 245.2 jit_solution(11382273469017339097)
XLA Ops:
  7.7 9.3 %collective-permute-done.15.refs_0_ = bf16[128,2048]{1,0:T(8,128)(2,1)S(1)} collective-permute-done((bf16[128,2048]{1,0:T(8,128)(2,1)S(1)}, bf16[128,2048]{1,0:T(8,128)(2,1)S(1)}, u32[]{:S(2)}, u32[]{:S(2)}) %collective-permute-start.15) | collective-permute-done | bytes 524320 | tf_op jit(solution)/shard_map/ppermute | solution.py:293
  18.9 11.8 %collective-permute-done.16.refs_0_ = bf16[128,2048]{1,0:T(8,128)(2,1)S(1)} collective-permute-done((bf16[128,2048]{1,0:T(8,128)(2,1)S(1)}, bf16[128,2048]{1,0:T(8,128)(2,1)S(1)}, u32[]{:S(2)}, u32[]{:S(2)}) %collective-permute-start.16) | collective-permute-done | bytes 524320 | tf_op jit(solution)/shard_map/ppermute | solution.py:293
  33.6 10.1 %collective-permute-done.17.refs_0_ = bf16[128,2048]{1,0:T(8,128)(2,1)} collective-permute-done((bf16[128,2048]{1,0:T(8,128)(2,1)S(1)}, bf16[128,2048]{1,0:T(8,128)(2,1)}, u32[]{:S(2)}, u32[]{:S(2)}) %collective-permute-start.17) | collective-permute-done | bytes 524320 | tf_op jit(solution)/shard_map/ppermute | solution.py:293
  46.6 9.4 %collective-permute-done.18.refs_0_ = bf16[128,2048]{1,0:T(8,128)(2,1)} collective-permute-done((bf16[128,2048]{1,0:T(8,128)(2,1)}, bf16[128,2048]{1,0:T(8,128)(2,1)}, u32[]{:S(2)}, u32[]{:S(2)}) %collective-permute-start.18) | collective-permute-done | bytes 524320 | tf_op jit(solution)/shard_map/ppermute | solution.py:293
  56.0 4.6 %copy-done = bf16[24,256,1024]{2,1,0:T(8,128)(2,1)S(1)} copy-done((bf16[24,256,1024]{2,1,0:T(8,128)(2,1)S(1)}, bf16[24,256,1024]{2,1,0:T(8,128)(2,1)}, u32[]{:S(2)}) %copy-start) | copy-done | bytes 12582936
  60.5 3.9 %attend.25 = bf16[128,2176]{1,0:T(8,128)(2,1)S(1)} custom-call(s32[36]{0:T(128)S(1)} %squeeze.8.plan_ref, bf16[128,2048]{1,0:T(8,128)(2,1)} %collective-permute-done.18.refs_0_, bf16[24,256,1024]{2,1,0:T(8,128)(2,1)S(1)} %copy-done, bf16[24,256,1024]{2,1,0:T(8,128)(2,1)} %collective-permute-done.refs_2_), custom_call_target="tpu_custom_call" | custom-call | flops 1073741824 | bytes 3211264 | tf_op jit(solution)/shard_map/attend/pallas_call | solution.py:140
  71.5 8.6 %collective-permute-done.19.refs_3_.refs_4_ = bf16[128,2176]{1,0:T(8,128)(2,1)S(1)} collective-permute-done((bf16[128,2176]{1,0:T(8,128)(2,1)S(1)}, bf16[128,2176]{1,0:T(8,128)(2,1)S(1)}, u32[]{:S(2)}, u32[]{:S(2)}) %collective-permute-start.19) | collective-permute-done | bytes 557088 | tf_op jit(solution)/shard_map/ppermute | solution.py:307
  80.1 4.1 %attend.26 = bf16[128,2176]{1,0:T(8,128)(2,1)S(1)} custom-call(s32[36]{0:T(128)S(1)} %squeeze.8.plan_ref, bf16[128,2048]{1,0:T(8,128)(2,1)} %collective-permute-done.17.refs_0_, bf16[24,256,1024]{2,1,0:T(8,128)(2,1)S(1)} %copy-done, bf16[24,256,1024]{2,1,0:T(8,128)(2,1)} %collective-permute-done.refs_2_, ...), custom_call_target="tpu_custom_call" | custom-call | flops 1073741824 | bytes 3211264 | tf_op jit(solution)/shard_map/attend/pallas_call | solution.py:140
  86.3 5.0 %collective-permute-done.8.refs_0_ = bf16[128,2048]{1,0:T(8,128)(2,1)S(1)} collective-permute-done((bf16[128,2048]{1,0:T(8,128)(2,1)S(1)}, bf16[128,2048]{1,0:T(8,128)(2,1)S(1)}, u32[]{:S(2)}, u32[]{:S(2)}) %collective-permute-start.8) | collective-permute-done | bytes 524320 | tf_op jit(solution)/shard_map/ppermute | solution.py:293
  92.3 4.1 %attend.30 = bf16[128,2176]{1,0:T(8,128)(2,1)S(1)} custom-call(s32[36]{0:T(128)S(1)} %squeeze.8.plan_ref, bf16[128,2048]{1,0:T(8,128)(2,1)} %collective-permute-done.24.refs_0_, bf16[24,256,1024]{2,1,0:T(8,128)(2,1)S(1)} %copy-done, bf16[24,256,1024]{2,1,0:T(8,128)(2,1)} %collective-permute-done.refs_2_, ...), custom_call_target="tpu_custom_call" | custom-call | flops 1073741824 | bytes 3211264 | tf_op jit(solution)/shard_map/attend/pallas_call | solution.py:140
  97.5 5.7 %collective-permute-done.20.refs_3_.refs_4_ = bf16[128,2176]{1,0:T(8,128)(2,1)S(1)} collective-permute-done((bf16[128,2176]{1,0:T(8,128)(2,1)S(1)}, bf16[128,2176]{1,0:T(8,128)(2,1)S(1)}, u32[]{:S(2)}, u32[]{:S(2)}) %collective-permute-start.20) | collective-permute-done | bytes 557088 | tf_op jit(solution)/shard_map/ppermute | solution.py:307
  103.2 4.0 %attend.27 = bf16[128,2176]{1,0:T(8,128)(2,1)S(1)} custom-call(s32[36]{0:T(128)S(1)} %squeeze.8.plan_ref, bf16[128,2048]{1,0:T(8,128)(2,1)S(1)} %copy-done.11, bf16[24,256,1024]{2,1,0:T(8,128)(2,1)S(1)} %copy-done, bf16[24,256,1024]{2,1,0:T(8,128)(2,1)} %collective-permute-done.refs_2_, bf16[128,2176]{1,0:T(8,128)(2,1)S(1)} %collective-permute-done.20.refs_3_.refs_4_, ...), custom_call_target="tpu_custom_call" | custom-call | flops 1073741824 | bytes 3211264 | tf_op jit(solution)/shard_map/attend/pallas_call | solution.py:140
  109.4 5.2 %collective-permute-done.9.refs_0_ = bf16[128,2048]{1,0:T(8,128)(2,1)} collective-permute-done((bf16[128,2048]{1,0:T(8,128)(2,1)S(1)}, bf16[128,2048]{1,0:T(8,128)(2,1)}, u32[]{:S(2)}, u32[]{:S(2)}) %collective-permute-start.9) | collective-permute-done | bytes 524320 | tf_op jit(solution)/shard_map/ppermute | solution.py:293
  115.6 4.0 %attend.31 = bf16[128,2176]{1,0:T(8,128)(2,1)S(1)} custom-call(s32[36]{0:T(128)S(1)} %squeeze.8.plan_ref, bf16[128,2048]{1,0:T(8,128)(2,1)S(1)} %collective-permute-done.23.refs_0_, bf16[24,256,1024]{2,1,0:T(8,128)(2,1)S(1)} %copy-done, bf16[24,256,1024]{2,1,0:T(8,128)(2,1)} %collective-permute-done.refs_2_, ...), custom_call_target="tpu_custom_call" | custom-call | flops 1073741824 | bytes 3211264 | tf_op jit(solution)/shard_map/attend/pallas_call | solution.py:140
  120.7 5.7 %collective-permute-done.21.refs_3_.refs_4_ = bf16[128,2176]{1,0:T(8,128)(2,1)S(1)} collective-permute-done((bf16[128,2176]{1,0:T(8,128)(2,1)S(1)}, bf16[128,2176]{1,0:T(8,128)(2,1)S(1)}, u32[]{:S(2)}, u32[]{:S(2)}) %collective-permute-start.21) | collective-permute-done | bytes 557088 | tf_op jit(solution)/shard_map/ppermute | solution.py:307
  126.4 4.0 %attend.28 = bf16[128,2176]{1,0:T(8,128)(2,1)S(1)} custom-call(s32[36]{0:T(128)S(1)} %squeeze.8.plan_ref, bf16[128,2048]{1,0:T(8,128)(2,1)S(1)} %collective-permute-done.15.refs_0_, bf16[24,256,1024]{2,1,0:T(8,128)(2,1)S(1)} %copy-done, bf16[24,256,1024]{2,1,0:T(8,128)(2,1)} %collective-permute-done.refs_2_, ...), custom_call_target="tpu_custom_call" | custom-call | flops 1073741824 | bytes 3211264 | tf_op jit(solution)/shard_map/attend/pallas_call | solution.py:140
  137.7 4.6 %copy-done.1 = bf16[24,256,1024]{2,1,0:T(8,128)(2,1)S(1)} copy-done((bf16[24,256,1024]{2,1,0:T(8,128)(2,1)S(1)}, bf16[24,256,1024]{2,1,0:T(8,128)(2,1)}, u32[]{:S(2)}) %copy-start.1) | copy-done | bytes 12582936
  142.3 3.9 %attend.20 = bf16[128,2176]{1,0:T(8,128)(2,1)S(1)} custom-call(s32[36]{0:T(128)S(1)} %squeeze.7.plan_ref, bf16[128,2048]{1,0:T(8,128)(2,1)} %collective-permute-done.10.refs_0_, bf16[24,256,1024]{2,1,0:T(8,128)(2,1)S(1)} %copy-done.1, bf16[24,256,1024]{2,1,0:T(8,128)(2,1)} %collective-permute-done.refs_2_), custom_call_target="tpu_custom_call" | custom-call | flops 1073741824 | bytes 3211264 | tf_op jit(solution)/shard_map/attend/pallas_call | solution.py:140
  147.4 4.6 %copy-done.2 = bf16[24,256,1024]{2,1,0:T(8,128)(2,1)S(1)} copy-done((bf16[24,256,1024]{2,1,0:T(8,128)(2,1)S(1)}, bf16[24,256,1024]{2,1,0:T(8,128)(2,1)}, u32[]{:S(2)}) %copy-start.2) | copy-done | bytes 12582936
  151.9 4.0 %attend.24.refs_0_ = bf16[128,2176]{1,0:T(8,128)(2,1)S(1)} custom-call(s32[36]{0:T(128)S(1)} %squeeze.8.plan_ref, bf16[128,2048]{1,0:T(8,128)(2,1)S(1)} %get-tuple-element.9.refs_0_, bf16[24,256,1024]{2,1,0:T(8,128)(2,1)S(1)} %copy-done.2, bf16[24,256,1024]{2,1,0:T(8,128)(2,1)} %collective-permute-done.refs_2_, bf16[128,1024]{1,0:T(8,128)(2,1)S(1)} %get-tuple-element.11.refs_3_), custom_call_target="tpu_custom_call" | custom-call | flops 1342177280 | bytes 3735552 | tf_op jit(solution)/shard_map/attend/pallas_call | solution.py:140
  155.9 14.6 %project.2 = bf16[128,8192]{1,0:T(8,128)(2,1)S(1)} custom-call(bf16[128,2176]{1,0:T(8,128)(2,1)S(1)} %attend.24.refs_0_, bf16[128,2176]{1,0:T(8,128)(2,1)S(1)} %collective-permute-done.22.refs_1_, bf16[128,2176]{1,0:T(8,128)(2,1)S(1)} %collective-permute-done.28.refs_2_, bf16[2048,8192]{1,0:T(8,128)(2,1)} %refs_6_.3, bf16[2048,8192]{1,0:T(8,128)(2,1)} %refs_6_.3, ...), custom_call_target="tpu_custom_call" | custom-call | flops 4294967296 | bytes 37748736 | tf_op jit(solution)/shard_map/project/pallas_call | solution.py:217
  172.2 4.6 %copy-done.3 = bf16[24,256,1024]{2,1,0:T(8,128)(2,1)S(1)} copy-done((bf16[24,256,1024]{2,1,0:T(8,128)(2,1)S(1)}, bf16[24,256,1024]{2,1,0:T(8,128)(2,1)}, u32[]{:S(2)}) %copy-start.3) | copy-done | bytes 12582936
  181.1 4.1 %attend.21 = bf16[128,2176]{1,0:T(8,128)(2,1)S(1)} custom-call(s32[36]{0:T(128)S(1)} %squeeze.7.plan_ref, bf16[128,2048]{1,0:T(8,128)(2,1)} %collective-permute-done.9.refs_0_, bf16[24,256,1024]{2,1,0:T(8,128)(2,1)S(1)} %copy-done.3, bf16[24,256,1024]{2,1,0:T(8,128)(2,1)} %collective-permute-done.refs_2_, ...), custom_call_target="tpu_custom_call" | custom-call | flops 1073741824 | bytes 3211264 | tf_op jit(solution)/shard_map/attend/pallas_call | solution.py:140
  186.8 6.0 %collective-permute-done.4.refs_3_.refs_4_ = bf16[128,2176]{1,0:T(8,128)(2,1)S(1)} collective-permute-done((bf16[128,2176]{1,0:T(8,128)(2,1)S(1)}, bf16[128,2176]{1,0:T(8,128)(2,1)S(1)}, u32[]{:S(2)}, u32[]{:S(2)}) %collective-permute-start.4) | collective-permute-done | bytes 557088 | tf_op jit(solution)/shard_map/ppermute | solution.py:307
  192.8 4.1 %attend.18 = bf16[128,2176]{1,0:T(8,128)(2,1)S(1)} custom-call(s32[36]{0:T(128)S(1)} %squeeze.7.plan_ref, bf16[128,2048]{1,0:T(8,128)(2,1)} %collective-permute-done.2.refs_0_, bf16[24,256,1024]{2,1,0:T(8,128)(2,1)S(1)} %copy-done.3, bf16[24,256,1024]{2,1,0:T(8,128)(2,1)} %collective-permute-done.refs_2_, ...), custom_call_target="tpu_custom_call" | custom-call | flops 1073741824 | bytes 3211264 | tf_op jit(solution)/shard_map/attend/pallas_call | solution.py:140
  197.7 4.0 %attend.22 = bf16[128,2176]{1,0:T(8,128)(2,1)S(1)} custom-call(s32[36]{0:T(128)S(1)} %squeeze.7.plan_ref, bf16[128,2048]{1,0:T(8,128)(2,1)S(1)} %copy-done.9, bf16[24,256,1024]{2,1,0:T(8,128)(2,1)S(1)} %copy-done.3, bf16[24,256,1024]{2,1,0:T(8,128)(2,1)} %collective-permute-done.refs_2_, bf16[128,2176]{1,0:T(8,128)(2,1)S(1)} %collective-permute-done.12.refs_3_.refs_4_, ...), custom_call_target="tpu_custom_call" | custom-call | flops 1073741824 | bytes 3211264 | tf_op jit(solution)/shard_map/attend/pallas_call | solution.py:140
  203.4 6.3 %collective-permute-done.5.refs_3_.refs_4_ = bf16[128,2176]{1,0:T(8,128)(2,1)S(1)} collective-permute-done((bf16[128,2176]{1,0:T(8,128)(2,1)S(1)}, bf16[128,2176]{1,0:T(8,128)(2,1)S(1)}, u32[]{:S(2)}, u32[]{:S(2)}) %collective-permute-start.5) | collective-permute-done | bytes 557088 | tf_op jit(solution)/shard_map/ppermute | solution.py:307
  209.7 4.1 %attend.19 = bf16[128,2176]{1,0:T(8,128)(2,1)S(1)} custom-call(s32[36]{0:T(128)S(1)} %squeeze.7.plan_ref, bf16[128,2048]{1,0:T(8,128)(2,1)} %collective-permute-done.1.refs_0_, bf16[24,256,1024]{2,1,0:T(8,128)(2,1)S(1)} %copy-done.3, bf16[24,256,1024]{2,1,0:T(8,128)(2,1)} %collective-permute-done.refs_2_, ...), custom_call_target="tpu_custom_call" | custom-call | flops 1073741824 | bytes 3211264 | tf_op jit(solution)/shard_map/attend/pallas_call | solution.py:140
  215.1 4.0 %attend.23 = bf16[128,2176]{1,0:T(8,128)(2,1)S(1)} custom-call(s32[36]{0:T(128)S(1)} %squeeze.7.plan_ref, bf16[128,2048]{1,0:T(8,128)(2,1)S(1)} %copy-done.7, bf16[24,256,1024]{2,1,0:T(8,128)(2,1)S(1)} %copy-done.3, bf16[24,256,1024]{2,1,0:T(8,128)(2,1)} %collective-permute-done.refs_2_, bf16[128,2176]{1,0:T(8,128)(2,1)S(1)} %collective-permute-done.13.refs_3_.refs_4_, ...), custom_call_target="tpu_custom_call" | custom-call | flops 1073741824 | bytes 3211264 | tf_op jit(solution)/shard_map/attend/pallas_call | solution.py:140
  220.8 4.6 %copy-done.4 = bf16[24,256,1024]{2,1,0:T(8,128)(2,1)S(1)} copy-done((bf16[24,256,1024]{2,1,0:T(8,128)(2,1)S(1)}, bf16[24,256,1024]{2,1,0:T(8,128)(2,1)}, u32[]{:S(2)}) %copy-start.4) | copy-done | bytes 12582936
  225.4 4.0 %attend.16.refs_0_ = bf16[128,2176]{1,0:T(8,128)(2,1)S(1)} custom-call(s32[36]{0:T(128)S(1)} %squeeze.7.plan_ref, bf16[128,2048]{1,0:T(8,128)(2,1)S(1)} %get-tuple-element.10.refs_0_, bf16[24,256,1024]{2,1,0:T(8,128)(2,1)S(1)} %copy-done.4, bf16[24,256,1024]{2,1,0:T(8,128)(2,1)} %collective-permute-done.refs_2_, bf16[128,1024]{1,0:T(8,128)(2,1)S(1)} %get-tuple-element.12.refs_3_), custom_call_target="tpu_custom_call" | custom-call | flops 1342177280 | bytes 3735552 | tf_op jit(solution)/shard_map/attend/pallas_call | solution.py:140
  229.5 15.7 %project.3 = bf16[128,8192]{1,0:T(8,128)(2,1)} custom-call(bf16[128,2176]{1,0:T(8,128)(2,1)S(1)} %attend.16.refs_0_, bf16[128,2176]{1,0:T(8,128)(2,1)S(1)} %collective-permute-done.6.refs_1_, bf16[128,2176]{1,0:T(8,128)(2,1)S(1)} %collective-permute-done.14.refs_2_, bf16[2048,8192]{1,0:T(8,128)(2,1)} %refs_6_.3, bf16[2048,8192]{1,0:T(8,128)(2,1)} %refs_6_.3, ...), custom_call_target="tpu_custom_call" | custom-call | flops 4294967296 | bytes 37748736 | tf_op jit(solution)/shard_map/project/pallas_call | solution.py:217
  (102 shorter events, 51.5 us)
Async XLA Ops:
  0.0 32.4 %copy-start.12 = (s32[8]{0:T(128)S(1)}, s32[8]{0:T(128)}, u32[]{:S(2)}) copy-start(s32[8]{0:T(128)} %constant.40.clone) | copy-start | bytes 100
  0.0 55.9 %collective-permute-start = (bf16[24,256,1024]{2,1,0:T(8,128)(2,1)}, bf16[24,256,1024]{2,1,0:T(8,128)(2,1)}, u32[]{:S(2)}, u32[]{:S(2)}) collective-permute-start(bf16[24,256,1024]{2,1,0:T(8,128)(2,1)} %refs_1_.31), channel_id=1, source_target_pairs={{0,2},{2,0},{4,6},{6,4},{8,10},{10,8},{12,14},{14,12},{16,18},{18,... | collective-permute-start | bytes 37748744 | tf_op jit(solution)/shard_map/ppermute | solution.py:278
  1.8 15.2 %collective-permute-start.15 = (bf16[128,2048]{1,0:T(8,128)(2,1)S(1)}, bf16[128,2048]{1,0:T(8,128)(2,1)S(1)}, u32[]{:S(2)}, u32[]{:S(2)}) collective-permute-start(bf16[128,2048]{1,0:T(8,128)(2,1)S(1)} %get-tuple-element.9.refs_0_), channel_id=1, source_target_pairs={{0,8},{2,10},{8,16},{10,18},{16,24},{18,26},{24,28},{26,30},{28,20... | collective-permute-start | bytes 1572872 | tf_op jit(solution)/shard_map/ppermute | solution.py:293
  4.5 28.7 %collective-permute-start.23 = (bf16[128,2048]{1,0:T(8,128)(2,1)S(1)}, bf16[128,2048]{1,0:T(8,128)(2,1)S(1)}, u32[]{:S(2)}, u32[]{:S(2)}) collective-permute-start(bf16[128,2048]{1,0:T(8,128)(2,1)S(1)} %get-tuple-element.9.refs_0_), channel_id=1, source_target_pairs={{8,0},{10,2},{16,8},{18,10},{24,16},{26,18},{28,24},{30,26},{20,28... | collective-permute-start | bytes 1572872 | tf_op jit(solution)/shard_map/ppermute | solution.py:293
  4.5 61.1 %collective-permute-start.7 = (bf16[128,2048]{1,0:T(8,128)(2,1)S(1)}, bf16[128,2048]{1,0:T(8,128)(2,1)S(1)}, u32[]{:S(2)}, u32[]{:S(2)}) collective-permute-start(bf16[128,2048]{1,0:T(8,128)(2,1)S(1)} %get-tuple-element.10.refs_0_), channel_id=1, source_target_pairs={{8,0},{10,2},{16,8},{18,10},{24,16},{26,18},{28,24},{30,26},{20,28... | collective-permute-start | bytes 1572872 | tf_op jit(solution)/shard_map/ppermute | solution.py:293
  17.0 13.7 %collective-permute-start.16 = (bf16[128,2048]{1,0:T(8,128)(2,1)S(1)}, bf16[128,2048]{1,0:T(8,128)(2,1)S(1)}, u32[]{:S(2)}, u32[]{:S(2)}) collective-permute-start(bf16[128,2048]{1,0:T(8,128)(2,1)S(1)} %collective-permute-done.15.refs_0_), channel_id=1, source_target_pairs={{0,8},{2,10},{8,16},{10,18},{16,24},{18,26},{24,28},{26,30},{28,20... | collective-permute-start | bytes 1572872 | tf_op jit(solution)/shard_map/ppermute | solution.py:293
  30.7 33.7 %copy-start.10 = (bf16[128,2048]{1,0:T(8,128)(2,1)}, bf16[128,2048]{1,0:T(8,128)(2,1)S(1)}, u32[]{:S(2)}) copy-start(bf16[128,2048]{1,0:T(8,128)(2,1)S(1)} %collective-permute-done.16.refs_0_) | copy-start | bytes 1572868
  30.7 13.0 %collective-permute-start.17 = (bf16[128,2048]{1,0:T(8,128)(2,1)S(1)}, bf16[128,2048]{1,0:T(8,128)(2,1)}, u32[]{:S(2)}, u32[]{:S(2)}) collective-permute-start(bf16[128,2048]{1,0:T(8,128)(2,1)S(1)} %collective-permute-done.16.refs_0_), channel_id=1, source_target_pairs={{0,8},{2,10},{8,16},{10,18},{16,24},{18,26},{24,28},{26,30},{28,20... | collective-permute-start | bytes 1572872 | tf_op jit(solution)/shard_map/ppermute | solution.py:293
  33.2 12.7 %collective-permute-start.24 = (bf16[128,2048]{1,0:T(8,128)(2,1)S(1)}, bf16[128,2048]{1,0:T(8,128)(2,1)}, u32[]{:S(2)}, u32[]{:S(2)}) collective-permute-start(bf16[128,2048]{1,0:T(8,128)(2,1)S(1)} %collective-permute-done.23.refs_0_), channel_id=1, source_target_pairs={{8,0},{10,2},{16,8},{18,10},{24,16},{26,18},{28,24},{30,26},{20,28... | collective-permute-start | bytes 1572872 | tf_op jit(solution)/shard_map/ppermute | solution.py:293
  43.7 12.3 %collective-permute-start.18 = (bf16[128,2048]{1,0:T(8,128)(2,1)}, bf16[128,2048]{1,0:T(8,128)(2,1)}, u32[]{:S(2)}, u32[]{:S(2)}) collective-permute-start(bf16[128,2048]{1,0:T(8,128)(2,1)} %collective-permute-done.17.refs_0_), channel_id=1, source_target_pairs={{0,8},{2,10},{8,16},{10,18},{16,24},{18,26},{24,28},{26,30},{28,20... | collective-permute-start | bytes 1572872 | tf_op jit(solution)/shard_map/ppermute | solution.py:293
  45.9 21.3 %collective-permute-start.25 = (bf16[128,2048]{1,0:T(8,128)(2,1)}, bf16[128,2048]{1,0:T(8,128)(2,1)S(1)}, u32[]{:S(2)}, u32[]{:S(2)}) collective-permute-start(bf16[128,2048]{1,0:T(8,128)(2,1)} %collective-permute-done.24.refs_0_), channel_id=1, source_target_pairs={{8,0},{10,2},{16,8},{18,10},{24,16},{26,18},{28,24},{30,26},{20,28... | collective-permute-start | bytes 1572872 | tf_op jit(solution)/shard_map/ppermute | solution.py:293
  64.4 15.6 %collective-permute-start.19 = (bf16[128,2176]{1,0:T(8,128)(2,1)S(1)}, bf16[128,2176]{1,0:T(8,128)(2,1)S(1)}, u32[]{:S(2)}, u32[]{:S(2)}) collective-permute-start(bf16[128,2176]{1,0:T(8,128)(2,1)S(1)} %attend.25), channel_id=1, source_target_pairs={{8,0},{10,2},{16,8},{18,10},{24,16},{26,18},{28,24},{30,26},{20,28... | collective-permute-start | bytes 1671176 | tf_op jit(solution)/shard_map/ppermute | solution.py:307
  65.5 25.7 %collective-permute-start.8 = (bf16[128,2048]{1,0:T(8,128)(2,1)S(1)}, bf16[128,2048]{1,0:T(8,128)(2,1)S(1)}, u32[]{:S(2)}, u32[]{:S(2)}) collective-permute-start(bf16[128,2048]{1,0:T(8,128)(2,1)S(1)} %collective-permute-done.7.refs_0_), channel_id=1, source_target_pairs={{8,0},{10,2},{16,8},{18,10},{24,16},{26,18},{28,24},{30,26},{20,28... | collective-permute-start | bytes 1572872 | tf_op jit(solution)/shard_map/ppermute | solution.py:293
  71.0 21.4 %collective-permute-start.26 = (bf16[128,2176]{1,0:T(8,128)(2,1)S(1)}, bf16[128,2176]{1,0:T(8,128)(2,1)S(1)}, u32[]{:S(2)}, u32[]{:S(2)}) collective-permute-start(bf16[128,2176]{1,0:T(8,128)(2,1)S(1)} %attend.29), channel_id=1, source_target_pairs={{0,8},{2,10},{8,16},{10,18},{16,24},{18,26},{24,28},{26,30},{28,20... | collective-permute-start | bytes 1671176 | tf_op jit(solution)/shard_map/ppermute | solution.py:307
  84.2 19.1 %collective-permute-start.20 = (bf16[128,2176]{1,0:T(8,128)(2,1)S(1)}, bf16[128,2176]{1,0:T(8,128)(2,1)S(1)}, u32[]{:S(2)}, u32[]{:S(2)}) collective-permute-start(bf16[128,2176]{1,0:T(8,128)(2,1)S(1)} %attend.26), channel_id=1, source_target_pairs={{8,0},{10,2},{16,8},{18,10},{24,16},{26,18},{28,24},{30,26},{20,28... | collective-permute-start | bytes 1671176 | tf_op jit(solution)/shard_map/ppermute | solution.py:307
  85.3 23.1 %collective-permute-start.1 = (bf16[128,2048]{1,0:T(8,128)(2,1)S(1)}, bf16[128,2048]{1,0:T(8,128)(2,1)}, u32[]{:S(2)}, u32[]{:S(2)}) collective-permute-start(bf16[128,2048]{1,0:T(8,128)(2,1)S(1)} %get-tuple-element.10.refs_0_), channel_id=1, source_target_pairs={{0,8},{2,10},{8,16},{10,18},{16,24},{18,26},{24,28},{26,30},{28,20... | collective-permute-start | bytes 1572872 | tf_op jit(solution)/shard_map/ppermute | solution.py:293
  91.3 23.3 %collective-permute-start.9 = (bf16[128,2048]{1,0:T(8,128)(2,1)S(1)}, bf16[128,2048]{1,0:T(8,128)(2,1)}, u32[]{:S(2)}, u32[]{:S(2)}) collective-permute-start(bf16[128,2048]{1,0:T(8,128)(2,1)S(1)} %collective-permute-done.8.refs_0_), channel_id=1, source_target_pairs={{8,0},{10,2},{16,8},{18,10},{24,16},{26,18},{28,24},{30,26},{20,28... | collective-permute-start | bytes 1572872 | tf_op jit(solution)/shard_map/ppermute | solution.py:293
  96.5 19.2 %collective-permute-start.27 = (bf16[128,2176]{1,0:T(8,128)(2,1)S(1)}, bf16[128,2176]{1,0:T(8,128)(2,1)S(1)}, u32[]{:S(2)}, u32[]{:S(2)}) collective-permute-start(bf16[128,2176]{1,0:T(8,128)(2,1)S(1)} %attend.30), channel_id=1, source_target_pairs={{0,8},{2,10},{8,16},{10,18},{16,24},{18,26},{24,28},{26,30},{28,20... | collective-permute-start | bytes 1671176 | tf_op jit(solution)/shard_map/ppermute | solution.py:307
  107.3 19.1 %collective-permute-start.21 = (bf16[128,2176]{1,0:T(8,128)(2,1)S(1)}, bf16[128,2176]{1,0:T(8,128)(2,1)S(1)}, u32[]{:S(2)}, u32[]{:S(2)}) collective-permute-start(bf16[128,2176]{1,0:T(8,128)(2,1)S(1)} %attend.27), channel_id=1, source_target_pairs={{8,0},{10,2},{16,8},{18,10},{24,16},{26,18},{28,24},{30,26},{20,28... | collective-permute-start | bytes 1671176 | tf_op jit(solution)/shard_map/ppermute | solution.py:307
  108.4 24.3 %collective-permute-start.2 = (bf16[128,2048]{1,0:T(8,128)(2,1)}, bf16[128,2048]{1,0:T(8,128)(2,1)}, u32[]{:S(2)}, u32[]{:S(2)}) collective-permute-start(bf16[128,2048]{1,0:T(8,128)(2,1)} %collective-permute-done.1.refs_0_), channel_id=1, source_target_pairs={{0,8},{2,10},{8,16},{10,18},{16,24},{18,26},{24,28},{26,30},{28,20... | collective-permute-start | bytes 1572872 | tf_op jit(solution)/shard_map/ppermute | solution.py:293
  114.6 23.2 %collective-permute-start.10 = (bf16[128,2048]{1,0:T(8,128)(2,1)}, bf16[128,2048]{1,0:T(8,128)(2,1)}, u32[]{:S(2)}, u32[]{:S(2)}) collective-permute-start(bf16[128,2048]{1,0:T(8,128)(2,1)} %collective-permute-done.9.refs_0_), channel_id=1, source_target_pairs={{8,0},{10,2},{16,8},{18,10},{24,16},{26,18},{28,24},{30,26},{20,28... | collective-permute-start | bytes 1572872 | tf_op jit(solution)/shard_map/ppermute | solution.py:293
  119.7 36.3 %collective-permute-start.28 = (bf16[128,2176]{1,0:T(8,128)(2,1)S(1)}, bf16[128,2176]{1,0:T(8,128)(2,1)S(1)}, u32[]{:S(2)}, u32[]{:S(2)}) collective-permute-start(bf16[128,2176]{1,0:T(8,128)(2,1)S(1)} %attend.31), channel_id=1, source_target_pairs={{0,8},{2,10},{8,16},{10,18},{16,24},{18,26},{24,28},{26,30},{28,20... | collective-permute-start | bytes 1671176 | tf_op jit(solution)/shard_map/ppermute | solution.py:307
  130.5 25.5 %collective-permute-start.22 = (bf16[128,2176]{1,0:T(8,128)(2,1)S(1)}, bf16[128,2176]{1,0:T(8,128)(2,1)S(1)}, u32[]{:S(2)}, u32[]{:S(2)}) collective-permute-start(bf16[128,2176]{1,0:T(8,128)(2,1)S(1)} %attend.28), channel_id=1, source_target_pairs={{8,0},{10,2},{16,8},{18,10},{24,16},{26,18},{28,24},{30,26},{20,28... | collective-permute-start | bytes 1671176 | tf_op jit(solution)/shard_map/ppermute | solution.py:307
  132.7 39.4 %collective-permute-start.3 = (bf16[128,2048]{1,0:T(8,128)(2,1)}, bf16[128,2048]{1,0:T(8,128)(2,1)S(1)}, u32[]{:S(2)}, u32[]{:S(2)}) collective-permute-start(bf16[128,2048]{1,0:T(8,128)(2,1)} %collective-permute-done.2.refs_0_), channel_id=1, source_target_pairs={{0,8},{2,10},{8,16},{10,18},{16,24},{18,26},{24,28},{26,30},{28,20... | collective-permute-start | bytes 1572872 | tf_op jit(solution)/shard_map/ppermute | solution.py:293
  146.2 34.9 %collective-permute-start.11 = (bf16[128,2176]{1,0:T(8,128)(2,1)S(1)}, bf16[128,2176]{1,0:T(8,128)(2,1)S(1)}, u32[]{:S(2)}, u32[]{:S(2)}) collective-permute-start(bf16[128,2176]{1,0:T(8,128)(2,1)S(1)} %attend.20), channel_id=1, source_target_pairs={{0,8},{2,10},{8,16},{10,18},{16,24},{18,26},{24,28},{26,30},{28,20... | collective-permute-start | bytes 1671176 | tf_op jit(solution)/shard_map/ppermute | solution.py:307
  170.6 58.9 %collective-permute-start.29 = (bf16[128,8192]{1,0:T(8,128)(2,1)S(1)}, bf16[128,8192]{1,0:T(8,128)(2,1)S(1)}, u32[]{:S(2)}, u32[]{:S(2)}) collective-permute-start(bf16[128,8192]{1,0:T(8,128)(2,1)S(1)} %project.2), channel_id=1, source_target_pairs={{0,1},{1,0},{2,3},{3,2},{4,5},{5,4},{6,7},{7,6},{8,9},{9,8},{10,11... | collective-permute-start | bytes 6291464 | tf_op jit(solution)/shard_map/ppermute | solution.py:314
  180.6 12.2 %collective-permute-start.4 = (bf16[128,2176]{1,0:T(8,128)(2,1)S(1)}, bf16[128,2176]{1,0:T(8,128)(2,1)S(1)}, u32[]{:S(2)}, u32[]{:S(2)}) collective-permute-start(bf16[128,2176]{1,0:T(8,128)(2,1)S(1)} %attend.17), channel_id=1, source_target_pairs={{8,0},{10,2},{16,8},{18,10},{24,16},{26,18},{28,24},{30,26},{20,28... | collective-permute-start | bytes 1671176 | tf_op jit(solution)/shard_map/ppermute | solution.py:307
  185.2 12.5 %collective-permute-start.12 = (bf16[128,2176]{1,0:T(8,128)(2,1)S(1)}, bf16[128,2176]{1,0:T(8,128)(2,1)S(1)}, u32[]{:S(2)}, u32[]{:S(2)}) collective-permute-start(bf16[128,2176]{1,0:T(8,128)(2,1)S(1)} %attend.21), channel_id=1, source_target_pairs={{0,8},{2,10},{8,16},{10,18},{16,24},{18,26},{24,28},{26,30},{28,20... | collective-permute-start | bytes 1671176 | tf_op jit(solution)/shard_map/ppermute | solution.py:307
  196.9 12.8 %collective-permute-start.5 = (bf16[128,2176]{1,0:T(8,128)(2,1)S(1)}, bf16[128,2176]{1,0:T(8,128)(2,1)S(1)}, u32[]{:S(2)}, u32[]{:S(2)}) collective-permute-start(bf16[128,2176]{1,0:T(8,128)(2,1)S(1)} %attend.18), channel_id=1, source_target_pairs={{8,0},{10,2},{16,8},{18,10},{24,16},{26,18},{28,24},{30,26},{20,28... | collective-permute-start | bytes 1671176 | tf_op jit(solution)/shard_map/ppermute | solution.py:307
  201.8 13.3 %collective-permute-start.13 = (bf16[128,2176]{1,0:T(8,128)(2,1)S(1)}, bf16[128,2176]{1,0:T(8,128)(2,1)S(1)}, u32[]{:S(2)}, u32[]{:S(2)}) collective-permute-start(bf16[128,2176]{1,0:T(8,128)(2,1)S(1)} %attend.22), channel_id=1, source_target_pairs={{0,8},{2,10},{8,16},{10,18},{16,24},{18,26},{24,28},{26,30},{28,20... | collective-permute-start | bytes 1671176 | tf_op jit(solution)/shard_map/ppermute | solution.py:307
  213.8 15.7 %collective-permute-start.6 = (bf16[128,2176]{1,0:T(8,128)(2,1)S(1)}, bf16[128,2176]{1,0:T(8,128)(2,1)S(1)}, u32[]{:S(2)}, u32[]{:S(2)}) collective-permute-start(bf16[128,2176]{1,0:T(8,128)(2,1)S(1)} %attend.19), channel_id=1, source_target_pairs={{8,0},{10,2},{16,8},{18,10},{24,16},{26,18},{28,24},{30,26},{20,28... | collective-permute-start | bytes 1671176 | tf_op jit(solution)/shard_map/ppermute | solution.py:307
  219.2 10.3 %collective-permute-start.14 = (bf16[128,2176]{1,0:T(8,128)(2,1)S(1)}, bf16[128,2176]{1,0:T(8,128)(2,1)S(1)}, u32[]{:S(2)}, u32[]{:S(2)}) collective-permute-start(bf16[128,2176]{1,0:T(8,128)(2,1)S(1)} %attend.23), channel_id=1, source_target_pairs={{0,8},{2,10},{8,16},{10,18},{16,24},{18,26},{24,28},{26,30},{28,20... | collective-permute-start | bytes 1671176 | tf_op jit(solution)/shard_map/ppermute | solution.py:307
  (16 other events, 164.2 us)
